TPU v7x, 32 devices: a whole 2x2x4 slice. The times are simulated.
32 devices in a mesh: group: 4 (over x, core), mp: 8 (over z, y).
Axes of the slice: x: 2, y: 2, z: 4, core: 2. Of those that a mesh axis runs over, the one named last changes fastest.
Arguments:
- arrivals: bfloat16 [4096, 2048], P(('group', 'mp')), may hold values from -6 to 6
- slots: int32 [4096], P(('group', 'mp')), may hold values from 0 to 1023, as said below
- lengths: int32 [4, 3], P('group'), may hold values from 1 to 768, 1024 in all within a row
- w_joined: float32 [2048, 1536], P('mp', 'group')
- w_expand: float32 [512, 2048], P('mp', 'group'), may hold values from -0.25 to 0.25
Outputs:
- attended: bfloat16 [4096, 1024], P(('group', 'mp'))
Inputs may be any that keep to these rules, and one draw needn't show every extreme that they name: `slots`: within each group the entries form a permutation of 0 to 1023; the 128 entries of one device hold exactly 8 values of every aligned run of 64 values.
All inputs are finite; a program needn't handle non-finite values.
Results may differ from a plain program's by a relative error of at most 0.03.
The roundings to bfloat16 on the way count: a program that leaves them out, or rounds other values in their place, can miss the bound.
Values may be sent and summed in bfloat16 or wider, within the bound.
No kernel may reach another device: no remote copies, remote signals or barrier semaphores. Data moves between devices by JAX's collectives and lax.ppermute only.
A program may use at most 64 MiB of HBM per device.

v0:
```python
import functools

import jax
import jax.numpy as jnp
from jax import lax
from jax.experimental import pallas as pl
from jax.experimental.pallas import tpu as pltpu
from jax.sharding import PartitionSpec as P

HEADS = 8
HDIM = 128
QCOLS = HEADS * HDIM

EPS = 1e-06
NEGATIVE = -1e30
LOG2_E = 1.4426950408889634
TILE = 16
NORM_COST = 64
VMEM = pl.BlockSpec(memory_space=pltpu.VMEM)
SMEM = pl.BlockSpec(memory_space=pltpu.SMEM)


def grant(mib):
    return pltpu.CompilerParams(vmem_limit_bytes=mib * 1024 * 1024)


def row_norm(values):
    mean_sq = jnp.mean(values * values, axis=-1, keepdims=True)
    return values * lax.rsqrt(mean_sq + EPS)


def ring_pairs(count, step):
    order = [2 * r if r < count // 2 else 2 * (count - 1 - r) + 1 for r in range(count)]
    return [(order[r], order[(r + step) % count]) for r in range(count)]


def ring_gather(block, count):
    up, down = ring_pairs(count, 1), ring_pairs(count, -1)
    below = above = block
    blocks = [block]
    for _ in range((count - 1) // 2):
        below, above = lax.ppermute(below, "mp", up), lax.ppermute(above, "mp", down)
        blocks += [below, above]
    cut = -(-block.shape[0] // 32) * 16
    return blocks + [lax.ppermute(below[:cut], "mp", up), lax.ppermute(above[cut:], "mp", down)]


def split_ring_gather(block, count, size, beside):
    up, down = ring_pairs(count, 1), ring_pairs(count, -1)
    below = above = block
    blocks = [block]
    for _ in range((count - 1) // 2):
        below, above = lax.ppermute(below, "mp", up), lax.ppermute(above, "mp", down)
        blocks += [below, above]
    made = beside(blocks)
    below, above, made = lax.optimization_barrier((below, above, made))
    last = jnp.where(lax.axis_index("group") % 2 == 0, below, above)
    pairs = [
        (group * count + source, group * count + target)
        for group in range(size)
        for source, target in (down if group % 2 else up)
    ]
    return blocks + [lax.ppermute(last, ("group", "mp"), pairs)], made


def ring_owners(count):
    me = lax.axis_index("mp")
    place = jnp.where(me % 2 == 0, me // 2, count - 1 - me // 2)
    owners = [me]
    for step in range(1, count // 2 + 1):
        for shift in (-step, step):
            at = lax.rem(place + shift + count, count)
            owners.append(jnp.where(at < count // 2, 2 * at, 2 * (count - 1 - at) + 1))
    return owners[:count]


def row_ranges(blocks):
    last = len(blocks) - 2
    return [(i, 0) for i in range(last + 1)] + [(last, blocks[last].shape[0])]


def group_gather(block, size, after=None):
    blocks = {0: block}
    bit = size // 2
    while bit:
        pairs = [(i, i ^ bit) for i in range(size)]
        for k in list(blocks):
            sent = blocks[k]
            if k and after is not None:
                sent, _ = lax.optimization_barrier((sent, after))
            blocks[k ^ bit] = lax.ppermute(sent, "group", pairs)
        bit //= 2
    return [blocks[k] for k in range(size)]


def pack_kernel(joined, expand, out):
    columns, high = joined.shape[1], expand.shape[0]
    folds = joined.shape[0] // high
    fold = expand.shape[1] // folds
    out[:, :columns] = joined[...].astype(jnp.bfloat16)
    for i in range(folds):
        out[i * high : (i + 1) * high, columns:] = expand[:, i * fold : (i + 1) * fold].astype(jnp.bfloat16)


def norm_kernel(arrivals, slots, normed, digits):
    normed[...] = row_norm(arrivals[...].astype(jnp.float32)).astype(jnp.bfloat16)
    rows = slots.shape[1]
    bits = jnp.concatenate([slots[...] & 255, slots[...] >> 8], axis=0).astype(jnp.float32)
    bits = jnp.concatenate([bits, jnp.zeros((14, rows), jnp.float32)], axis=0)
    digits[...] = jnp.zeros_like(digits)
    digits[:, :rows] = bits.astype(jnp.bfloat16)


def multiply(tokens, starts, blocks, columns):
    total = None
    for start, block in zip(starts, blocks):
        span = pl.ds(pl.multiple_of(start, 128), block.shape[0])
        left = jnp.concatenate([token[:, span] for token in tokens], axis=0)
        product = jnp.dot(left, block[:, :columns], preferred_element_type=jnp.float32)
        total = product if total is None else total + product
    return total


def early_kernel(count, size, *refs):
    tokens, blocks, total = refs[:size], refs[size:-1], refs[-1]
    depth = blocks[0].shape[0]
    total[...] = multiply(tokens, [owner * depth for owner in ring_owners(count)], blocks, total.shape[1])


def proj_kernel(count, size, early, *refs):
    tokens, refs = refs[:size], refs[size:]
    blocks, refs = refs[: count + 1], refs[count + 1 :]
    depth = blocks[0].shape[0]
    owners = ring_owners(count)
    starts = [owners[i] * depth + offset for i, offset in row_ranges(blocks)]
    if early:
        total, refs = refs[0], refs[1:]
        outs, expand = refs[:size], refs[size]
        rows, columns = outs[0].shape
        proj = total[...] + multiply(tokens, starts[early:], blocks[early:], columns)
    else:
        outs, expand, weight = refs[:size], refs[size], refs[size + 1]
        rows, columns = outs[0].shape
        for start, block in zip(starts, blocks):
            length = block.shape[0]
            weight[pl.ds(pl.multiple_of(start, length), length), :] = block[:, :columns]
        products = [jnp.dot(token[...], weight[...], preferred_element_type=jnp.float32) for token in tokens]
        proj = jnp.concatenate(products, axis=0)
    at = lax.axis_index("group") * columns + lax.broadcasted_iota(jnp.int32, (1, columns), 1)
    proj = proj * jnp.where(at < QCOLS, HDIM**-0.5, 1.0).astype(jnp.float32)
    for i, out in enumerate(outs):
        out[...] = proj[i * rows : (i + 1) * rows].astype(jnp.bfloat16)
    high = expand.shape[0] // count
    for i, owner in enumerate(owners):
        parts = []
        for block in blocks[i:] if i == count - 1 else blocks[i : i + 1]:
            parts += [block[j * high : (j + 1) * high, columns:] for j in range(block.shape[0] // high)]
        expand[pl.ds(pl.multiple_of(owner * high, high), high), :] = jnp.concatenate(parts, axis=1)


def assemble_kernel(size, digits, *refs):
    products, (query, block, proj) = refs[:size], refs[size:]
    group = lax.axis_index("group")
    for i, product in enumerate(products):
        proj[group ^ i] = product[...]
    whole = jnp.concatenate([proj[i] for i in range(size)], axis=1)
    query[...] = whole[:, :QCOLS]
    rows = query.shape[0]
    block[:rows] = row_norm(whole[:, QCOLS:].astype(jnp.float32)).astype(jnp.bfloat16)
    block[rows:] = digits[...]


def position_of(block, rows):
    digits = block[block.shape[0] - 16 :, :rows].astype(jnp.float32)
    return digits[1:2] * 256.0 + digits[:1]


def bias_of(lengths, own, others):
    rows = own.shape[0] - 16
    same = lax.broadcasted_iota(jnp.int32, (rows, rows), 0) == lax.broadcasted_iota(jnp.int32, (rows, rows), 1)
    position = jnp.sum(jnp.where(same, position_of(own, rows), 0.0), axis=1, keepdims=True).astype(jnp.int32)
    start = jnp.zeros_like(position)
    end = 0
    for i in range(lengths.shape[1]):
        end = end + lengths[0, i]
        start = jnp.where(position >= end, end, start)
    others = others.astype(jnp.int32)
    return jnp.where((others <= position) & (others >= start), 0.0, NEGATIVE)


def score(turned, latent, scores):
    half = turned.shape[0] // 2
    for at in (0, half):
        scores[at : at + half] = lax.dot_general(
            turned[at : at + half], latent[...], (((1,), (1,)), ((), ())), preferred_element_type=jnp.float32
        )


def start_kernel(count, size, lengths, query, *refs):
    blocks, refs = refs[: count - 3], refs[count - 3 :]
    expands, refs = refs[:size], refs[size:]
    turned, value, peaks, sums, summed, latent, expand, scores, probs = refs
    rows = query.shape[0]
    for i, block in enumerate(blocks):
        latent[i * rows : (i + 1) * rows, :] = block[:rows]
    bias = bias_of(lengths, blocks[0], jnp.concatenate([position_of(block, rows) for block in blocks], axis=1))
    width = expands[0].shape[1]
    for i, block in enumerate(expands):
        at = (lax.axis_index("group") ^ i) * width
        expand[:, pl.ds(pl.multiple_of(at, width), width)] = block[...]
    for head in range(HEADS):
        value[:, head * HDIM : (head + 1) * HDIM] = expand[:, (2 * head + 1) * HDIM : (2 * head + 2) * HDIM]
        product = lax.dot_general(
            query[:, head * HDIM : (head + 1) * HDIM],
            expand[:, head * 2 * HDIM : (2 * head + 1) * HDIM],
            (((1,), (1,)), ((), ())),
            preferred_element_type=jnp.float32,
        )
        turned[head * rows : (head + 1) * rows] = (product * LOG2_E).astype(jnp.bfloat16)
    score(turned, latent, scores)
    half = HEADS * rows // 2
    for begin in (0, half):
        for at in range(begin, begin + half, TILE):
            here = at % rows
            part = scores[at : at + TILE] + bias[here : here + TILE]
            peak = jnp.max(part, axis=-1, keepdims=True)
            weights = jnp.exp2(part - peak)
            peaks[at : at + TILE] = jnp.broadcast_to(peak, (TILE, HDIM))
            sums[at : at + TILE] = jnp.broadcast_to(jnp.sum(weights, axis=-1, keepdims=True), (TILE, HDIM))
            probs[at : at + TILE] = weights.astype(jnp.bfloat16)
        summed[begin : begin + half] = jnp.dot(
            probs[begin : begin + half], latent[...], preferred_element_type=jnp.float32
        )


def absorb(biases, scores, peaks, sums):
    part = scores + biases
    peak = jnp.maximum(peaks, jnp.max(part, axis=-1, keepdims=True))
    weights = jnp.exp2(part - jnp.concatenate([peak] * (part.shape[1] // HDIM), axis=1))
    factor = jnp.exp2(peaks - peak)
    return weights.astype(jnp.bfloat16), factor, peak, sums * factor + jnp.sum(weights, axis=-1, keepdims=True)


def more_kernel(lengths, own, turned, value, peaks, sums, summed, *refs):
    blocks, (new_peaks, new_sums, outcome, latent, scores) = refs[:-5], refs[-5:]
    rows, some = own.shape[0] - 16, HEADS // 2
    for i, block in enumerate(blocks):
        latent[i * rows : (i + 1) * rows, :] = block[:rows]
    bias = bias_of(lengths, own, jnp.concatenate([position_of(block, rows) for block in blocks], axis=1))
    biases = jnp.concatenate([bias] * some, axis=0)
    score(turned, latent, scores)
    for first in range(0, HEADS, some):
        here = slice(first * rows, (first + some) * rows)
        probs, factor, new_peaks[here], new_sums[here] = absorb(biases, scores[here], peaks[here], sums[here])
        update = jnp.dot(probs, latent[...], preferred_element_type=jnp.float32)
        update = update + summed[here] * jnp.concatenate([factor] * (summed.shape[1] // HDIM), axis=1)
        update = update.astype(jnp.bfloat16)
        for i in range(some):
            head = first + i
            outcome[head * rows : (head + 1) * rows] = jnp.dot(
                update[i * rows : (i + 1) * rows],
                value[:, head * HDIM : (head + 1) * HDIM],
                preferred_element_type=jnp.float32,
            )


def attend_kernel(lengths, own, turned, value, peaks, sums, before, last, out, scores):
    rows = out.shape[0]
    latent = last[:rows]
    bias = bias_of(lengths, own, position_of(last, rows))
    score(turned, latent, scores)
    values = jnp.dot(latent, value[...], preferred_element_type=jnp.float32).astype(jnp.bfloat16)
    some = HEADS // 2
    biases = jnp.concatenate([bias] * some, axis=0)
    for first in range(0, HEADS, some):
        here = slice(first * rows, (first + some) * rows)
        probs, factor, _, total = absorb(biases, scores[here], peaks[here], sums[here])
        kept = before[here] * factor
        for i in range(some):
            columns = slice((first + i) * HDIM, (first + i + 1) * HDIM)
            mine = slice(i * rows, (i + 1) * rows)
            outcome = kept[mine] + jnp.dot(probs[mine], values[:, columns], preferred_element_type=jnp.float32)
            out[:, columns] = (outcome / total[mine]).astype(jnp.bfloat16)


def body(arrivals, slots, lengths, w_joined, w_expand):
    count, size = lax.axis_size("mp"), lax.axis_size("group")
    rows, depth = arrivals.shape
    columns, rank = w_joined.shape[1], w_expand.shape[0] * count
    own_columns = w_expand.shape[1]

    weights = pl.pallas_call(
        pack_kernel,
        out_shape=jax.ShapeDtypeStruct(
            (w_joined.shape[0], columns + own_columns * w_expand.shape[0] // w_joined.shape[0]), jnp.bfloat16
        ),
        in_specs=[VMEM, VMEM],
        out_specs=VMEM,
        compiler_params=grant(16),
        name="pack",
    )(w_joined, w_expand)
    blocks = ring_gather(weights, count)
    arrivals, _ = lax.optimization_barrier((arrivals, weights))
    normed, digits = pl.pallas_call(
        norm_kernel,
        out_shape=[
            jax.ShapeDtypeStruct((rows, depth), jnp.bfloat16),
            jax.ShapeDtypeStruct((16, rank), jnp.bfloat16),
        ],
        in_specs=[VMEM, VMEM],
        out_specs=[VMEM, VMEM],
        compiler_params=grant(16),
        cost_estimate=pl.CostEstimate(flops=NORM_COST * rows * depth, bytes_accessed=NORM_COST * rows * depth, transcendentals=rows),
        name="norm",
    )(arrivals, slots.reshape(1, rows))
    tokens = group_gather(normed, size, blocks[-4:-2])
    early = 0 if w_joined.shape[0] // 2 % 128 else count - 3
    total = []
    if early:
        total = [
            pl.pallas_call(
                functools.partial(early_kernel, count, size),
                out_shape=jax.ShapeDtypeStruct((size * rows, columns), jnp.float32),
                in_specs=[VMEM] * (size + early),
                out_specs=VMEM,
                compiler_params=grant(16),
                cost_estimate=pl.CostEstimate(
                    flops=2 * size * rows * depth * columns, bytes_accessed=4 * depth * columns, transcendentals=0
                ),
                name="project_early",
            )(*tokens, *blocks[:early])
        ]
    *projs, own_expand = pl.pallas_call(
        functools.partial(proj_kernel, count, size, early),
        out_shape=[jax.ShapeDtypeStruct((rows, columns), jnp.bfloat16)] * size
        + [jax.ShapeDtypeStruct((rank, own_columns), jnp.bfloat16)],
        in_specs=[VMEM] * (size + count + 1 + len(total)),
        out_specs=[VMEM] * (size + 1),
        scratch_shapes=[] if early else [pltpu.VMEM((depth, columns), jnp.bfloat16)],
        compiler_params=grant(16),
        cost_estimate=pl.CostEstimate(
            flops=2 * size * rows * depth * columns, bytes_accessed=4 * depth * columns, transcendentals=0
        ),
        name="project",
    )(*tokens, *blocks, *total)

    back = [projs[0]]
    for k in range(1, size):
        back.append(lax.ppermute(projs[k], "group", [(i, i ^ k) for i in range(size)]))
    own_expand, _ = lax.optimization_barrier((own_expand, back[1:]))
    query, block = pl.pallas_call(
        functools.partial(assemble_kernel, size),
        out_shape=[
            jax.ShapeDtypeStruct((rows, QCOLS), jnp.bfloat16),
            jax.ShapeDtypeStruct((rows + 16, rank), jnp.bfloat16),
        ],
        in_specs=[VMEM] * (size + 1),
        out_specs=[VMEM, VMEM],
        scratch_shapes=[pltpu.VMEM((size, rows, columns), jnp.bfloat16)],
        compiler_params=grant(16),
        name="assemble",
    )(digits, *back)
    total, early = count * rows, count - 3
    needed = grant(8 + total * HEADS * rows * 8 // (1024 * 1024))
    state = [jax.ShapeDtypeStruct((HEADS * rows, width), jnp.float32) for width in (HDIM, HDIM, rank)]

    def cost(blocks):
        return pl.CostEstimate(
            flops=4 * blocks * rows * rank * QCOLS,
            bytes_accessed=8 * QCOLS * rank,
            transcendentals=HEADS * rows * blocks * rows,
        )

    def attend_start(blocks):
        expands = group_gather(own_expand, size, blocks[3:5])
        return pl.pallas_call(
            functools.partial(start_kernel, count, size),
            out_shape=[
                jax.ShapeDtypeStruct((HEADS * rows, rank), jnp.bfloat16),
                jax.ShapeDtypeStruct((rank, QCOLS), jnp.bfloat16),
                *state,
            ],
            in_specs=[SMEM] + [VMEM] * (1 + early + size),
            out_specs=[VMEM] * 5,
            scratch_shapes=[
                pltpu.VMEM((early * rows, rank), jnp.bfloat16),
                pltpu.VMEM((rank, 2 * QCOLS), jnp.bfloat16),
                pltpu.VMEM((HEADS * rows, early * rows), jnp.float32),
                pltpu.VMEM((HEADS * rows, early * rows), jnp.bfloat16),
            ],
            compiler_params=needed,
            cost_estimate=cost(early),
            name="attend_start",
        )(lengths, query, *blocks[:early], *expands)

    lat_blocks, (turned, value, *running) = split_ring_gather(block, count, size, attend_start)
    running = pl.pallas_call(
        more_kernel,
        out_shape=[jax.ShapeDtypeStruct((HEADS * rows, HDIM), jnp.float32)] * 3,
        in_specs=[SMEM] + [VMEM] * 8,
        out_specs=[VMEM] * 3,
        scratch_shapes=[
            pltpu.VMEM((2 * rows, rank), jnp.bfloat16),
            pltpu.VMEM((HEADS * rows, 2 * rows), jnp.float32),
        ],
        compiler_params=grant(16),
        cost_estimate=cost(2),
        name="attend_more",
    )(lengths, block, turned, value, *running, *lat_blocks[early : count - 1])
    return pl.pallas_call(
        attend_kernel,
        out_shape=jax.ShapeDtypeStruct((rows, QCOLS), jnp.bfloat16),
        in_specs=[SMEM] + [VMEM] * 7,
        out_specs=VMEM,
        scratch_shapes=[pltpu.VMEM((HEADS * rows, rows), jnp.float32)],
        compiler_params=grant(16),
        cost_estimate=cost(2),
        name="attend",
    )(lengths, block, turned, value, *running, lat_blocks[-1])


def solution(mesh):
    in_specs = (
        P(("group", "mp"), None),
        P(("group", "mp")),
        P("group", None),
        P("mp", "group"),
        P("mp", "group"),
    )
    out_specs = P(("group", "mp"), None)
    return jax.shard_map(body, mesh=mesh, in_specs=in_specs, out_specs=out_specs, check_vma=False)
```

profile of v0, /device:TPU:0, one launch (start us, length us, event | category | flops | bytes accessed | tf_op | source)
XLA Modules:
  0.0 69.5 jit_solution(7370158916671714300)
XLA Ops:
  1.9 3.1 %collective-permute-start.2 = (bf16[256,512]{1,0:T(8,128)(2,1)S(1)}, bf16[256,512]{1,0:T(8,128)(2,1)S(1)}, u32[]{:S(2)}, u32[]{:S(2)}) collective-permute-start(bf16[256,512]{1,0:T(8,128)(2,1)S(1)} %pack.1.refs_4_), channel_id=1, source_target_pairs={{0,2},{2,4},{4,6},{6,7},{7,5},{5,3},{3,1},{1,0},{8,10},{10,12},{12... | collective-permute-start | bytes 786440 | tf_op jit(solution)/shard_map/ppermute | solution.py:42
  6.9 2.0 %collective-permute-start.1 = (bf16[128,2048]{1,0:T(8,128)(2,1)S(1)}, bf16[128,2048]{1,0:T(8,128)(2,1)S(1)}, u32[]{:S(2)}, u32[]{:S(2)}) collective-permute-start(bf16[128,2048]{1,0:T(8,128)(2,1)S(1)} %get-tuple-element.35.refs_0_), channel_id=1, source_target_pairs={{0,16},{8,24},{16,0},{24,8},{1,17},{9,25},{17,1},{25,9},{2,18},{10... | collective-permute-start | bytes 1572872 | tf_op jit(solution)/shard_map/ppermute | solution.py:91
  8.9 2.3 %collective-permute-done.2.refs_5_ = bf16[256,512]{1,0:T(8,128)(2,1)S(1)} collective-permute-done((bf16[256,512]{1,0:T(8,128)(2,1)S(1)}, bf16[256,512]{1,0:T(8,128)(2,1)S(1)}, u32[]{:S(2)}, u32[]{:S(2)}) %collective-permute-start.2) | collective-permute-done | bytes 262176 | tf_op jit(solution)/shard_map/ppermute | solution.py:42
  11.3 1.8 %collective-permute-start.3 = (bf16[256,512]{1,0:T(8,128)(2,1)S(1)}, bf16[256,512]{1,0:T(8,128)(2,1)S(1)}, u32[]{:S(2)}, u32[]{:S(2)}) collective-permute-start(bf16[256,512]{1,0:T(8,128)(2,1)S(1)} %collective-permute-done.2.refs_5_), channel_id=1, source_target_pairs={{0,2},{2,4},{4,6},{6,7},{7,5},{5,3},{3,1},{1,0},{8,10},{10,12},{12... | collective-permute-start | bytes 786440 | tf_op jit(solution)/shard_map/ppermute | solution.py:42
  13.3 5.5 %collective-permute-done.3.refs_7_ = bf16[256,512]{1,0:T(8,128)(2,1)S(1)} collective-permute-done((bf16[256,512]{1,0:T(8,128)(2,1)S(1)}, bf16[256,512]{1,0:T(8,128)(2,1)S(1)}, u32[]{:S(2)}, u32[]{:S(2)}) %collective-permute-start.3) | collective-permute-done | bytes 262176 | tf_op jit(solution)/shard_map/ppermute | solution.py:42
  18.8 1.5 %collective-permute-start.4 = (bf16[256,512]{1,0:T(8,128)(2,1)S(1)}, bf16[256,512]{1,0:T(8,128)(2,1)S(1)}, u32[]{:S(2)}, u32[]{:S(2)}) collective-permute-start(bf16[256,512]{1,0:T(8,128)(2,1)S(1)} %collective-permute-done.3.refs_7_), channel_id=1, source_target_pairs={{0,2},{2,4},{4,6},{6,7},{7,5},{5,3},{3,1},{1,0},{8,10},{10,12},{12... | collective-permute-start | bytes 786440 | tf_op jit(solution)/shard_map/ppermute | solution.py:42
  20.8 4.5 %collective-permute-done.4.refs_9_ = bf16[256,512]{1,0:T(8,128)(2,1)S(1)} collective-permute-done((bf16[256,512]{1,0:T(8,128)(2,1)S(1)}, bf16[256,512]{1,0:T(8,128)(2,1)S(1)}, u32[]{:S(2)}, u32[]{:S(2)}) %collective-permute-start.4) | collective-permute-done | bytes 262176 | tf_op jit(solution)/shard_map/ppermute | solution.py:42
  27.2 1.5 %collective-permute-start.9 = (bf16[128,512]{1,0:T(8,128)(2,1)S(1)}, bf16[128,512]{1,0:T(8,128)(2,1)S(1)}, u32[]{:S(2)}, u32[]{:S(2)}) collective-permute-start(bf16[128,512]{1,0:T(8,128)(2,1)S(1)} %slice.8), channel_id=1, source_target_pairs={{0,2},{2,4},{4,6},{6,7},{7,5},{5,3},{3,1},{1,0},{8,10},{10,12},{12... | collective-permute-start | bytes 393224 | tf_op jit(solution)/shard_map/ppermute | solution.py:45
  29.6 2.9 %collective-permute-done.10.refs_12_ = bf16[128,512]{1,0:T(8,128)(2,1)S(1)} collective-permute-done((bf16[128,512]{1,0:T(8,128)(2,1)S(1)}, bf16[128,512]{1,0:T(8,128)(2,1)S(1)}, u32[]{:S(2)}, u32[]{:S(2)}) %collective-permute-start.10) | collective-permute-done | bytes 131104 | tf_op jit(solution)/shard_map/ppermute | solution.py:45
  33.7 1.5 %collective-permute-start.12 = (bf16[128,384]{1,0:T(8,128)(2,1)S(1)}, bf16[128,384]{1,0:T(8,128)(2,1)S(1)}, u32[]{:S(2)}, u32[]{:S(2)}) collective-permute-start(bf16[128,384]{1,0:T(8,128)(2,1)S(1)} %get-tuple-element.39), channel_id=1, source_target_pairs={{0,16},{8,24},{16,0},{24,8},{1,17},{9,25},{17,1},{25,9},{2,18},{10... | collective-permute-start | bytes 294920 | tf_op jit(solution)/shard_map/ppermute | solution.py:349
  35.6 3.8 %collective-permute-done.12.refs_2_ = bf16[128,384]{1,0:T(8,128)(2,1)S(1)} collective-permute-done((bf16[128,384]{1,0:T(8,128)(2,1)S(1)}, bf16[128,384]{1,0:T(8,128)(2,1)S(1)}, u32[]{:S(2)}, u32[]{:S(2)}) %collective-permute-start.12) | collective-permute-done | bytes 98336 | tf_op jit(solution)/shard_map/ppermute | solution.py:349
  40.6 1.4 %collective-permute-start.21 = (bf16[512,512]{1,0:T(8,128)(2,1)S(1)}, bf16[512,512]{1,0:T(8,128)(2,1)S(1)}, u32[]{:S(2)}, u32[]{:S(2)}) collective-permute-start(bf16[512,512]{1,0:T(8,128)(2,1)S(1)} %get-tuple-element.44.refs_5_), channel_id=1, source_target_pairs={{0,16},{8,24},{16,0},{24,8},{1,17},{9,25},{17,1},{25,9},{2,18},{10... | collective-permute-start | bytes 1572872 | tf_op jit(solution)/shard_map/ppermute | solution.py:91
  42.2 1.6 %collective-permute-start.14 = (bf16[144,512]{1,0:T(8,128)(2,1)S(1)}, bf16[144,512]{1,0:T(8,128)(2,1)S(1)}, u32[]{:S(2)}, u32[]{:S(2)}) collective-permute-start(bf16[144,512]{1,0:T(8,128)(2,1)S(1)} %get-tuple-element.41.refs_0_.own), channel_id=1, source_target_pairs={{0,2},{2,4},{4,6},{6,7},{7,5},{5,3},{3,1},{1,0},{8,10},{10,12},{12... | collective-permute-start | bytes 442376 | tf_op jit(solution)/shard_map/ppermute | solution.py:53
  44.2 3.7 %collective-permute-done.14.refs_1_ = bf16[144,512]{1,0:T(8,128)(2,1)S(1)} collective-permute-done((bf16[144,512]{1,0:T(8,128)(2,1)S(1)}, bf16[144,512]{1,0:T(8,128)(2,1)S(1)}, u32[]{:S(2)}, u32[]{:S(2)}) %collective-permute-start.14) | collective-permute-done | bytes 147488 | tf_op jit(solution)/shard_map/ppermute | solution.py:53
  48.0 1.6 %collective-permute-start.15 = (bf16[144,512]{1,0:T(8,128)(2,1)S(1)}, bf16[144,512]{1,0:T(8,128)(2,1)S(1)}, u32[]{:S(2)}, u32[]{:S(2)}) collective-permute-start(bf16[144,512]{1,0:T(8,128)(2,1)S(1)} %collective-permute-done.14.refs_1_), channel_id=1, source_target_pairs={{0,2},{2,4},{4,6},{6,7},{7,5},{5,3},{3,1},{1,0},{8,10},{10,12},{12... | collective-permute-start | bytes 442376 | tf_op jit(solution)/shard_map/ppermute | solution.py:53
  50.0 3.1 %collective-permute-done.15.refs_3_ = bf16[144,512]{1,0:T(8,128)(2,1)S(1)} collective-permute-done((bf16[144,512]{1,0:T(8,128)(2,1)S(1)}, bf16[144,512]{1,0:T(8,128)(2,1)S(1)}, u32[]{:S(2)}, u32[]{:S(2)}) %collective-permute-start.15) | collective-permute-done | bytes 147488 | tf_op jit(solution)/shard_map/ppermute | solution.py:53
  53.1 1.6 %collective-permute-done.18.refs_4_ = bf16[144,512]{1,0:T(8,128)(2,1)S(1)} collective-permute-done((bf16[144,512]{1,0:T(8,128)(2,1)S(1)}, bf16[144,512]{1,0:T(8,128)(2,1)S(1)}, u32[]{:S(2)}, u32[]{:S(2)}) %collective-permute-start.18) | collective-permute-done | bytes 147488 | tf_op jit(solution)/shard_map/ppermute | solution.py:53
  54.7 1.6 %collective-permute-start.16 = (bf16[144,512]{1,0:T(8,128)(2,1)S(1)}, bf16[144,512]{1,0:T(8,128)(2,1)S(1)}, u32[]{:S(2)}, u32[]{:S(2)}) collective-permute-start(bf16[144,512]{1,0:T(8,128)(2,1)S(1)} %collective-permute-done.15.refs_3_), channel_id=1, source_target_pairs={{0,2},{2,4},{4,6},{6,7},{7,5},{5,3},{3,1},{1,0},{8,10},{10,12},{12... | collective-permute-start | bytes 442376 | tf_op jit(solution)/shard_map/ppermute | solution.py:53
  56.7 3.4 %attend_start.1 = (bf16[1024,512]{1,0:T(8,128)(2,1)S(1)}, bf16[512,1024]{1,0:T(8,128)(2,1)S(1)}, f32[1024,128]{1,0:T(8,128)S(1)}, f32[1024,128]{1,0:T(8,128)S(1)}, f32[1024,512]{1,0:T(8,128)S(1)}) custom-call(s32[1,3]{1,0:T(1,128)S(1)} %copy-done.3, bf16[128,1024]{1,0:T(8,128)(2,1)S(1)} %get-tuple-element.42.query, ...), custom_call_target="tpu_custom_call" | custom-call | flops 1342177280 | bytes 4194304 | tf_op jit(solution)/shard_map/attend_start/pallas_call | solution.py:376
  61.0 1.3 %collective-permute-done.19.refs_1_ = bf16[144,512]{1,0:T(8,128)(2,1)S(1)} collective-permute-done((bf16[144,512]{1,0:T(8,128)(2,1)S(1)}, bf16[144,512]{1,0:T(8,128)(2,1)S(1)}, u32[]{:S(2)}, u32[]{:S(2)}) %collective-permute-start.19) | collective-permute-done | bytes 147488 | tf_op jit(solution)/shard_map/ppermute | solution.py:53
  62.3 1.6 %collective-permute-start.23 = (bf16[144,512]{1,0:T(8,128)(2,1)S(1)}, bf16[144,512]{1,0:T(8,128)(2,1)S(1)}, u32[]{:S(2)}, u32[]{:S(2)}) collective-permute-start(bf16[144,512]{1,0:T(8,128)(2,1)S(1)} %broadcast_select_fusion), channel_id=1, source_target_pairs={{0,2},{2,4},{4,6},{6,7},{7,5},{5,3},{3,1},{1,0},{8,9},{10,8},{12,1... | collective-permute-start | bytes 442376 | tf_op jit(solution)/shard_map/ppermute | solution.py:63
  63.9 2.2 %attend_more.1 = (f32[1024,128]{1,0:T(8,128)S(1)}, f32[1024,128]{1,0:T(8,128)S(1)}, f32[1024,128]{1,0:T(8,128)S(1)}) custom-call(s32[1,3]{1,0:T(1,128)S(1)} %copy-done.3, bf16[144,512]{1,0:T(8,128)(2,1)S(1)} %get-tuple-element.41.refs_0_.own, bf16[1024,512]{1,0:T(8,128)(2,1)S(1)} %get-tuple-element.51.turned, bf16[512,1024]{1,0:T(8,128)(2,1)S(1)} %get-tuple-element.52.value, ...), custom_call_target="tpu_custom_call" | custom-call | flops 536870912 | bytes 4194304 | tf_op jit(solution)/shard_map/attend_more/pallas_call | solution.py:397
  66.1 1.4 %collective-permute-done.23.last = bf16[144,512]{1,0:T(8,128)(2,1)S(1)} collective-permute-done((bf16[144,512]{1,0:T(8,128)(2,1)S(1)}, bf16[144,512]{1,0:T(8,128)(2,1)S(1)}, u32[]{:S(2)}, u32[]{:S(2)}) %collective-permute-start.23) | collective-permute-done | bytes 147488 | tf_op jit(solution)/shard_map/ppermute | solution.py:63
  67.5 2.1 %attend.1 = bf16[128,1024]{1,0:T(8,128)(2,1)} custom-call(s32[1,3]{1,0:T(1,128)S(1)} %copy-done.3, bf16[144,512]{1,0:T(8,128)(2,1)S(1)} %get-tuple-element.41.refs_0_.own, bf16[1024,512]{1,0:T(8,128)(2,1)S(1)} %get-tuple-element.51.turned, bf16[512,1024]{1,0:T(8,128)(2,1)S(1)} %get-tuple-element.52.value, f32[1024,128]{1,0:T(8,128)S(1)} %get-tuple-element.56.peaks, ...), custom_call_target="tpu_custom_call" | custom-call | flops 536870912 | bytes 4194304 | tf_op jit(solution)/shard_map/attend/pallas_call | solution.py:410
  (45 shorter events, 12.5 us)
Async XLA Ops:
  1.9 9.3 %collective-permute-start.2 = (bf16[256,512]{1,0:T(8,128)(2,1)S(1)}, bf16[256,512]{1,0:T(8,128)(2,1)S(1)}, u32[]{:S(2)}, u32[]{:S(2)}) collective-permute-start(bf16[256,512]{1,0:T(8,128)(2,1)S(1)} %pack.1.refs_4_), channel_id=1, source_target_pairs={{0,2},{2,4},{4,6},{6,7},{7,5},{5,3},{3,1},{1,0},{8,10},{10,12},{12... | collective-permute-start | bytes 786440 | tf_op jit(solution)/shard_map/ppermute | solution.py:42
  5.0 8.0 %collective-permute-start.5 = (bf16[256,512]{1,0:T(8,128)(2,1)S(1)}, bf16[256,512]{1,0:T(8,128)(2,1)S(1)}, u32[]{:S(2)}, u32[]{:S(2)}) collective-permute-start(bf16[256,512]{1,0:T(8,128)(2,1)S(1)} %pack.1.refs_4_), channel_id=1, source_target_pairs={{0,1},{2,0},{4,2},{6,4},{7,6},{5,7},{3,5},{1,3},{8,9},{10,8},{12,1... | collective-permute-start | bytes 786440 | tf_op jit(solution)/shard_map/ppermute | solution.py:42
  6.9 13.9 %collective-permute-start.1 = (bf16[128,2048]{1,0:T(8,128)(2,1)S(1)}, bf16[128,2048]{1,0:T(8,128)(2,1)S(1)}, u32[]{:S(2)}, u32[]{:S(2)}) collective-permute-start(bf16[128,2048]{1,0:T(8,128)(2,1)S(1)} %get-tuple-element.35.refs_0_), channel_id=1, source_target_pairs={{0,16},{8,24},{16,0},{24,8},{1,17},{9,25},{17,1},{25,9},{2,18},{10... | collective-permute-start | bytes 1572872 | tf_op jit(solution)/shard_map/ppermute | solution.py:91
  11.3 7.5 %collective-permute-start.3 = (bf16[256,512]{1,0:T(8,128)(2,1)S(1)}, bf16[256,512]{1,0:T(8,128)(2,1)S(1)}, u32[]{:S(2)}, u32[]{:S(2)}) collective-permute-start(bf16[256,512]{1,0:T(8,128)(2,1)S(1)} %collective-permute-done.2.refs_5_), channel_id=1, source_target_pairs={{0,2},{2,4},{4,6},{6,7},{7,5},{5,3},{3,1},{1,0},{8,10},{10,12},{12... | collective-permute-start | bytes 786440 | tf_op jit(solution)/shard_map/ppermute | solution.py:42
  13.1 7.2 %collective-permute-start.6 = (bf16[256,512]{1,0:T(8,128)(2,1)S(1)}, bf16[256,512]{1,0:T(8,128)(2,1)S(1)}, u32[]{:S(2)}, u32[]{:S(2)}) collective-permute-start(bf16[256,512]{1,0:T(8,128)(2,1)S(1)} %collective-permute-done.5.refs_6_), channel_id=1, source_target_pairs={{0,1},{2,0},{4,2},{6,4},{7,6},{5,7},{3,5},{1,3},{8,9},{10,8},{12,1... | collective-permute-start | bytes 786440 | tf_op jit(solution)/shard_map/ppermute | solution.py:42
  18.8 6.6 %collective-permute-start.4 = (bf16[256,512]{1,0:T(8,128)(2,1)S(1)}, bf16[256,512]{1,0:T(8,128)(2,1)S(1)}, u32[]{:S(2)}, u32[]{:S(2)}) collective-permute-start(bf16[256,512]{1,0:T(8,128)(2,1)S(1)} %collective-permute-done.3.refs_7_), channel_id=1, source_target_pairs={{0,2},{2,4},{4,6},{6,7},{7,5},{5,3},{3,1},{1,0},{8,10},{10,12},{12... | collective-permute-start | bytes 786440 | tf_op jit(solution)/shard_map/ppermute | solution.py:42
  20.2 6.4 %collective-permute-start.7 = (bf16[256,512]{1,0:T(8,128)(2,1)S(1)}, bf16[256,512]{1,0:T(8,128)(2,1)S(1)}, u32[]{:S(2)}, u32[]{:S(2)}) collective-permute-start(bf16[256,512]{1,0:T(8,128)(2,1)S(1)} %collective-permute-done.6.refs_8_), channel_id=1, source_target_pairs={{0,1},{2,0},{4,2},{6,4},{7,6},{5,7},{3,5},{1,3},{8,9},{10,8},{12,1... | collective-permute-start | bytes 786440 | tf_op jit(solution)/shard_map/ppermute | solution.py:42
  20.8 8.0 %collective-permute-start = (bf16[128,2048]{1,0:T(8,128)(2,1)S(1)}, bf16[128,2048]{1,0:T(8,128)(2,1)S(1)}, u32[]{:S(2)}, u32[]{:S(2)}) collective-permute-start(bf16[128,2048]{1,0:T(8,128)(2,1)S(1)} %get-tuple-element.35.refs_0_), channel_id=1, source_target_pairs={{0,8},{8,0},{16,24},{24,16},{1,9},{9,1},{17,25},{25,17},{2,10},{10... | collective-permute-start | bytes 1572872 | tf_op jit(solution)/shard_map/ppermute | solution.py:91
  26.6 2.2 %collective-permute-start.8 = (bf16[128,2048]{1,0:T(8,128)(2,1)S(1)}, bf16[128,2048]{1,0:T(8,128)(2,1)S(1)}, u32[]{:S(2)}, u32[]{:S(2)}) collective-permute-start(bf16[128,2048]{1,0:T(8,128)(2,1)S(1)} %collective-permute-done.1.refs_2_), channel_id=1, source_target_pairs={{0,8},{8,0},{16,24},{24,16},{1,9},{9,1},{17,25},{25,17},{2,10},{10... | collective-permute-start | bytes 1572872 | tf_op jit(solution)/shard_map/ppermute | solution.py:91
  26.6 6.0 %collective-permute-start.10 = (bf16[128,512]{1,0:T(8,128)(2,1)S(1)}, bf16[128,512]{1,0:T(8,128)(2,1)S(1)}, u32[]{:S(2)}, u32[]{:S(2)}) collective-permute-start(bf16[128,512]{1,0:T(8,128)(2,1)S(1)} %slice.9), channel_id=1, source_target_pairs={{0,1},{2,0},{4,2},{6,4},{7,6},{5,7},{3,5},{1,3},{8,9},{10,8},{12,1... | collective-permute-start | bytes 393224 | tf_op jit(solution)/shard_map/ppermute | solution.py:45
  27.2 5.7 %collective-permute-start.9 = (bf16[128,512]{1,0:T(8,128)(2,1)S(1)}, bf16[128,512]{1,0:T(8,128)(2,1)S(1)}, u32[]{:S(2)}, u32[]{:S(2)}) collective-permute-start(bf16[128,512]{1,0:T(8,128)(2,1)S(1)} %slice.8), channel_id=1, source_target_pairs={{0,2},{2,4},{4,6},{6,7},{7,5},{5,3},{3,1},{1,0},{8,10},{10,12},{12... | collective-permute-start | bytes 393224 | tf_op jit(solution)/shard_map/ppermute | solution.py:45
  33.6 1.9 %collective-permute-start.11 = (bf16[128,384]{1,0:T(8,128)(2,1)S(1)}, bf16[128,384]{1,0:T(8,128)(2,1)S(1)}, u32[]{:S(2)}, u32[]{:S(2)}) collective-permute-start(bf16[128,384]{1,0:T(8,128)(2,1)S(1)} %get-tuple-element.38), channel_id=1, source_target_pairs={{0,8},{8,0},{16,24},{24,16},{1,9},{9,1},{17,25},{25,17},{2,10},{10... | collective-permute-start | bytes 294920 | tf_op jit(solution)/shard_map/ppermute | solution.py:349
  33.7 5.7 %collective-permute-start.12 = (bf16[128,384]{1,0:T(8,128)(2,1)S(1)}, bf16[128,384]{1,0:T(8,128)(2,1)S(1)}, u32[]{:S(2)}, u32[]{:S(2)}) collective-permute-start(bf16[128,384]{1,0:T(8,128)(2,1)S(1)} %get-tuple-element.39), channel_id=1, source_target_pairs={{0,16},{8,24},{16,0},{24,8},{1,17},{9,25},{17,1},{25,9},{2,18},{10... | collective-permute-start | bytes 294920 | tf_op jit(solution)/shard_map/ppermute | solution.py:349
  35.2 5.4 %collective-permute-start.13 = (bf16[128,384]{1,0:T(8,128)(2,1)S(1)}, bf16[128,384]{1,0:T(8,128)(2,1)S(1)}, u32[]{:S(2)}, u32[]{:S(2)}) collective-permute-start(bf16[128,384]{1,0:T(8,128)(2,1)S(1)} %get-tuple-element.40), channel_id=1, source_target_pairs={{0,24},{8,16},{16,8},{24,0},{1,25},{9,17},{17,9},{25,1},{2,26},{10... | collective-permute-start | bytes 294920 | tf_op jit(solution)/shard_map/ppermute | solution.py:349
  40.6 14.1 %collective-permute-start.21 = (bf16[512,512]{1,0:T(8,128)(2,1)S(1)}, bf16[512,512]{1,0:T(8,128)(2,1)S(1)}, u32[]{:S(2)}, u32[]{:S(2)}) collective-permute-start(bf16[512,512]{1,0:T(8,128)(2,1)S(1)} %get-tuple-element.44.refs_5_), channel_id=1, source_target_pairs={{0,16},{8,24},{16,0},{24,8},{1,17},{9,25},{17,1},{25,9},{2,18},{10... | collective-permute-start | bytes 1572872 | tf_op jit(solution)/shard_map/ppermute | solution.py:91
  42.2 5.8 %collective-permute-start.14 = (bf16[144,512]{1,0:T(8,128)(2,1)S(1)}, bf16[144,512]{1,0:T(8,128)(2,1)S(1)}, u32[]{:S(2)}, u32[]{:S(2)}) collective-permute-start(bf16[144,512]{1,0:T(8,128)(2,1)S(1)} %get-tuple-element.41.refs_0_.own), channel_id=1, source_target_pairs={{0,2},{2,4},{4,6},{6,7},{7,5},{5,3},{3,1},{1,0},{8,10},{10,12},{12... | collective-permute-start | bytes 442376 | tf_op jit(solution)/shard_map/ppermute | solution.py:53
  43.8 5.8 %collective-permute-start.17 = (bf16[144,512]{1,0:T(8,128)(2,1)S(1)}, bf16[144,512]{1,0:T(8,128)(2,1)S(1)}, u32[]{:S(2)}, u32[]{:S(2)}) collective-permute-start(bf16[144,512]{1,0:T(8,128)(2,1)S(1)} %get-tuple-element.41.refs_0_.own), channel_id=1, source_target_pairs={{0,1},{2,0},{4,2},{6,4},{7,6},{5,7},{3,5},{1,3},{8,9},{10,8},{12,1... | collective-permute-start | bytes 442376 | tf_op jit(solution)/shard_map/ppermute | solution.py:53
  48.0 5.1 %collective-permute-start.15 = (bf16[144,512]{1,0:T(8,128)(2,1)S(1)}, bf16[144,512]{1,0:T(8,128)(2,1)S(1)}, u32[]{:S(2)}, u32[]{:S(2)}) collective-permute-start(bf16[144,512]{1,0:T(8,128)(2,1)S(1)} %collective-permute-done.14.refs_1_), channel_id=1, source_target_pairs={{0,2},{2,4},{4,6},{6,7},{7,5},{5,3},{3,1},{1,0},{8,10},{10,12},{12... | collective-permute-start | bytes 442376 | tf_op jit(solution)/shard_map/ppermute | solution.py:53
  49.5 5.1 %collective-permute-start.18 = (bf16[144,512]{1,0:T(8,128)(2,1)S(1)}, bf16[144,512]{1,0:T(8,128)(2,1)S(1)}, u32[]{:S(2)}, u32[]{:S(2)}) collective-permute-start(bf16[144,512]{1,0:T(8,128)(2,1)S(1)} %collective-permute-done.17.refs_2_), channel_id=1, source_target_pairs={{0,1},{2,0},{4,2},{6,4},{7,6},{5,7},{3,5},{1,3},{8,9},{10,8},{12,1... | collective-permute-start | bytes 442376 | tf_op jit(solution)/shard_map/ppermute | solution.py:53
  50.0 6.7 %collective-permute-start.20 = (bf16[512,512]{1,0:T(8,128)(2,1)S(1)}, bf16[512,512]{1,0:T(8,128)(2,1)S(1)}, u32[]{:S(2)}, u32[]{:S(2)}) collective-permute-start(bf16[512,512]{1,0:T(8,128)(2,1)S(1)} %get-tuple-element.44.refs_5_), channel_id=1, source_target_pairs={{0,8},{8,0},{16,24},{24,16},{1,9},{9,1},{17,25},{25,17},{2,10},{10... | collective-permute-start | bytes 1572872 | tf_op jit(solution)/shard_map/ppermute | solution.py:91
  54.7 2.0 %collective-permute-start.22 = (bf16[512,512]{1,0:T(8,128)(2,1)S(1)}, bf16[512,512]{1,0:T(8,128)(2,1)S(1)}, u32[]{:S(2)}, u32[]{:S(2)}) collective-permute-start(bf16[512,512]{1,0:T(8,128)(2,1)S(1)} %collective-permute-done.21.refs_7_), channel_id=1, source_target_pairs={{0,8},{8,0},{16,24},{24,16},{1,9},{9,1},{17,25},{25,17},{2,10},{10... | collective-permute-start | bytes 1572872 | tf_op jit(solution)/shard_map/ppermute | solution.py:91
  54.7 6.3 %collective-permute-start.16 = (bf16[144,512]{1,0:T(8,128)(2,1)S(1)}, bf16[144,512]{1,0:T(8,128)(2,1)S(1)}, u32[]{:S(2)}, u32[]{:S(2)}) collective-permute-start(bf16[144,512]{1,0:T(8,128)(2,1)S(1)} %collective-permute-done.15.refs_3_), channel_id=1, source_target_pairs={{0,2},{2,4},{4,6},{6,7},{7,5},{5,3},{3,1},{1,0},{8,10},{10,12},{12... | collective-permute-start | bytes 442376 | tf_op jit(solution)/shard_map/ppermute | solution.py:53
  56.3 6.0 %collective-permute-start.19 = (bf16[144,512]{1,0:T(8,128)(2,1)S(1)}, bf16[144,512]{1,0:T(8,128)(2,1)S(1)}, u32[]{:S(2)}, u32[]{:S(2)}) collective-permute-start(bf16[144,512]{1,0:T(8,128)(2,1)S(1)} %collective-permute-done.18.refs_4_), channel_id=1, source_target_pairs={{0,1},{2,0},{4,2},{6,4},{7,6},{5,7},{3,5},{1,3},{8,9},{10,8},{12,1... | collective-permute-start | bytes 442376 | tf_op jit(solution)/shard_map/ppermute | solution.py:53
  62.3 5.2 %collective-permute-start.23 = (bf16[144,512]{1,0:T(8,128)(2,1)S(1)}, bf16[144,512]{1,0:T(8,128)(2,1)S(1)}, u32[]{:S(2)}, u32[]{:S(2)}) collective-permute-start(bf16[144,512]{1,0:T(8,128)(2,1)S(1)} %broadcast_select_fusion), channel_id=1, source_target_pairs={{0,2},{2,4},{4,6},{6,7},{7,5},{5,3},{3,1},{1,0},{8,9},{10,8},{12,1... | collective-permute-start | bytes 442376 | tf_op jit(solution)/shard_map/ppermute | solution.py:63
  (5 other events, 30.7 us)
where the time goes:
time: 69.8 us; the launch traced here: 69.5 us
  waiting for transfers between devices  33.9 us (49%)
  starting transfers between devices  22.4 us (32%)
  Pallas kernels  9.54 us (14%)
  local copies, waits for them, and re-layouts  3.62 us (5%)
    ppermute x3, waiting for transfers between devices, ring_gather(): lax.ppermute(below, 'mp', up)  12.3 us
    ppermute x3, waiting for transfers between devices, split_ring_gather(): lax.ppermute(below, 'mp', up)  7.7 us
    ppermute x3, starting transfers between devices, ring_gather(): lax.ppermute(below, 'mp', up)  6.35 us
    ppermute x3, waiting for transfers between devices, body(): lax.ppermute(projs[k], 'group', [(i, i ^ k) for i in range(size)])  5 us
    ppermute x3, starting transfers between devices, split_ring_gather(): lax.ppermute(below, 'mp', up)  4.78 us
    unnamed x10, local copies, waits for them, and re-layouts  3.6 us
    ppermute x6, starting transfers between devices, group_gather(): blocks[k ^ bit] = lax.ppermute(sent, 'group', pairs)  3.41 us
    pallas_call x1, Pallas kernels, attend_start(): pl.pallas_call(functools.partial(start_kernel, count, size), out_shape=[j...  3.35 us
  transfers between devices with their start and end apart: 24, of which 14 were waited for; matrix products, arithmetic and copies ran while one was open for 0% of the time, Pallas kernels for 10%

commit v1 on v0

--- a/solution.py
+++ b/solution.py
@@ -34,26 +34,14 @@
     return [(order[r], order[(r + step) % count]) for r in range(count)]
 
 
-def ring_gather(block, count):
+def ring_gather(block, count, size, beside=lambda blocks: ()):
     up, down = ring_pairs(count, 1), ring_pairs(count, -1)
     below = above = block
     blocks = [block]
     for _ in range((count - 1) // 2):
         below, above = lax.ppermute(below, "mp", up), lax.ppermute(above, "mp", down)
         blocks += [below, above]
-    cut = -(-block.shape[0] // 32) * 16
-    return blocks + [lax.ppermute(below[:cut], "mp", up), lax.ppermute(above[cut:], "mp", down)]
-
-
-def split_ring_gather(block, count, size, beside):
-    up, down = ring_pairs(count, 1), ring_pairs(count, -1)
-    below = above = block
-    blocks = [block]
-    for _ in range((count - 1) // 2):
-        below, above = lax.ppermute(below, "mp", up), lax.ppermute(above, "mp", down)
-        blocks += [below, above]
-    made = beside(blocks)
-    below, above, made = lax.optimization_barrier((below, above, made))
+    below, above, made = lax.optimization_barrier((below, above, beside(blocks)))
     last = jnp.where(lax.axis_index("group") % 2 == 0, below, above)
     pairs = [
         (group * count + source, group * count + target)
@@ -72,11 +60,6 @@
             at = lax.rem(place + shift + count, count)
             owners.append(jnp.where(at < count // 2, 2 * at, 2 * (count - 1 - at) + 1))
     return owners[:count]
-
-
-def row_ranges(blocks):
-    last = len(blocks) - 2
-    return [(i, 0) for i in range(last + 1)] + [(last, blocks[last].shape[0])]
 
 
 def group_gather(block, size, after=None):
@@ -129,10 +112,10 @@
 
 def proj_kernel(count, size, early, *refs):
     tokens, refs = refs[:size], refs[size:]
-    blocks, refs = refs[: count + 1], refs[count + 1 :]
+    blocks, refs = refs[:count], refs[count:]
     depth = blocks[0].shape[0]
     owners = ring_owners(count)
-    starts = [owners[i] * depth + offset for i, offset in row_ranges(blocks)]
+    starts = [owner * depth for owner in owners]
     if early:
         total, refs = refs[0], refs[1:]
         outs, expand = refs[:size], refs[size]
@@ -151,10 +134,8 @@
     for i, out in enumerate(outs):
         out[...] = proj[i * rows : (i + 1) * rows].astype(jnp.bfloat16)
     high = expand.shape[0] // count
-    for i, owner in enumerate(owners):
-        parts = []
-        for block in blocks[i:] if i == count - 1 else blocks[i : i + 1]:
-            parts += [block[j * high : (j + 1) * high, columns:] for j in range(block.shape[0] // high)]
+    for owner, block in zip(owners, blocks):
+        parts = [block[i * high : (i + 1) * high, columns:] for i in range(depth // high)]
         expand[pl.ds(pl.multiple_of(owner * high, high), high), :] = jnp.concatenate(parts, axis=1)
 
 
@@ -299,7 +280,7 @@
         compiler_params=grant(16),
         name="pack",
     )(w_joined, w_expand)
-    blocks = ring_gather(weights, count)
+    blocks, _ = ring_gather(weights, count, size)
     arrivals, _ = lax.optimization_barrier((arrivals, weights))
     normed, digits = pl.pallas_call(
         norm_kernel,
@@ -313,8 +294,8 @@
         cost_estimate=pl.CostEstimate(flops=NORM_COST * rows * depth, bytes_accessed=NORM_COST * rows * depth, transcendentals=rows),
         name="norm",
     )(arrivals, slots.reshape(1, rows))
-    tokens = group_gather(normed, size, blocks[-4:-2])
-    early = 0 if w_joined.shape[0] // 2 % 128 else count - 3
+    tokens = group_gather(normed, size, blocks[-3:-1])
+    early = 0 if w_joined.shape[0] % 128 else count - 1
     total = []
     if early:
         total = [
@@ -334,7 +315,7 @@
         functools.partial(proj_kernel, count, size, early),
         out_shape=[jax.ShapeDtypeStruct((rows, columns), jnp.bfloat16)] * size
         + [jax.ShapeDtypeStruct((rank, own_columns), jnp.bfloat16)],
-        in_specs=[VMEM] * (size + count + 1 + len(total)),
+        in_specs=[VMEM] * (size + count + len(total)),
         out_specs=[VMEM] * (size + 1),
         scratch_shapes=[] if early else [pltpu.VMEM((depth, columns), jnp.bfloat16)],
         compiler_params=grant(16),
@@ -393,7 +374,7 @@
             name="attend_start",
         )(lengths, query, *blocks[:early], *expands)
 
-    lat_blocks, (turned, value, *running) = split_ring_gather(block, count, size, attend_start)
+    lat_blocks, (turned, value, *running) = ring_gather(block, count, size, attend_start)
     running = pl.pallas_call(
         more_kernel,
         out_shape=[jax.ShapeDtypeStruct((HEADS * rows, HDIM), jnp.float32)] * 3,

time: 69.8 us -> 70.4 us (level)
  local copies, waits for them, and re-layouts: 3.62 us -> 6.89 us
  waiting for transfers between devices: 33.9 us -> 31.8 us
    ppermute x9 -> x2, waiting for transfers between devices: 15.2 us -> 2.96 us  [ring_gather(): return (blocks + [lax.ppermute(last, ('group', 'mp'), pairs)], made)]
    ppermute x9 -> x2, starting transfers between devices: 9.9 us -> 3.2 us  [ring_gather(): return (blocks + [lax.ppermute(last, ('group', 'mp'), pairs)], made)]
    ppermute x3 -> x6, waiting for transfers between devices: 12.3 us -> 18.7 us  [ring_gather(): lax.ppermute(below, 'mp', up)]
    ppermute x3 -> x6, starting transfers between devices: 6.35 us -> 11.1 us  [ring_gather(): lax.ppermute(below, 'mp', up)]
    ppermute x3 -> x6, waiting for transfers between devices: 1.29 us -> 4.87 us  [ring_gather(): lax.ppermute(above, 'mp', down)]
    unnamed x10 -> x18, local copies, waits for them, and re-layouts: 3.6 us -> 6.89 us
    ppermute x3 -> x6, starting transfers between devices: 0.79 us -> 2.13 us  [ring_gather(): lax.ppermute(above, 'mp', down)]
  transfers between devices with their start and end apart: 24 -> 23, of which waited for: 14 -> 14; matrix products, arithmetic and copies ran while one was open for 0% -> 0% of each run, Pallas kernels for 10% -> 10%
where the time goes in v1:
time: 70.4 us; the launch traced here: 70.1 us
  waiting for transfers between devices  31.8 us (45%)
  starting transfers between devices  21.9 us (31%)
  Pallas kernels  9.4 us (13%)
  local copies, waits for them, and re-layouts  6.89 us (10%)
    ppermute x6, waiting for transfers between devices, ring_gather(): lax.ppermute(below, 'mp', up)  18.7 us
    ppermute x6, starting transfers between devices, ring_gather(): lax.ppermute(below, 'mp', up)  11.1 us
    unnamed x18, local copies, waits for them, and re-layouts  6.89 us
    ppermute x3, waiting for transfers between devices, body(): lax.ppermute(projs[k], 'group', [(i, i ^ k) for i in range(size)])  5 us
    ppermute x6, waiting for transfers between devices, ring_gather(): lax.ppermute(above, 'mp', down)  4.87 us
    ppermute x6, starting transfers between devices, group_gather(): blocks[k ^ bit] = lax.ppermute(sent, 'group', pairs)  3.5 us
    pallas_call x1, Pallas kernels, attend_start(): pl.pallas_call(functools.partial(start_kernel, count, size), out_shape=[j...  3.3 us
    ppermute x2, starting transfers between devices, ring_gather(): return (blocks + [lax.ppermute(last, ('group', 'mp'), pairs)], made)  3.2 us
  transfers between devices with their start and end apart: 23, of which 14 were waited for; matrix products, arithmetic and copies ran while one was open for 0% of the time, Pallas kernels for 10%

profile of v1, /device:TPU:0, one launch (start us, length us, event | category | flops | bytes accessed | tf_op | source)
XLA Modules:
  0.0 70.1 jit_solution(1332516578088332355)
XLA Ops:
  1.9 3.1 %collective-permute-start.2 = (bf16[256,512]{1,0:T(8,128)(2,1)S(1)}, bf16[256,512]{1,0:T(8,128)(2,1)S(1)}, u32[]{:S(2)}, u32[]{:S(2)}) collective-permute-start(bf16[256,512]{1,0:T(8,128)(2,1)S(1)} %pack.1.refs_4_), channel_id=1, source_target_pairs={{0,2},{2,4},{4,6},{6,7},{7,5},{5,3},{3,1},{1,0},{8,10},{10,12},{12... | collective-permute-start | bytes 786440 | tf_op jit(solution)/shard_map/ppermute | solution.py:42
  6.9 2.0 %collective-permute-start.1 = (bf16[128,2048]{1,0:T(8,128)(2,1)S(1)}, bf16[128,2048]{1,0:T(8,128)(2,1)S(1)}, u32[]{:S(2)}, u32[]{:S(2)}) collective-permute-start(bf16[128,2048]{1,0:T(8,128)(2,1)S(1)} %get-tuple-element.37.refs_0_), channel_id=1, source_target_pairs={{0,16},{8,24},{16,0},{24,8},{1,17},{9,25},{17,1},{25,9},{2,18},{10... | collective-permute-start | bytes 1572872 | tf_op jit(solution)/shard_map/ppermute | solution.py:74
  8.9 2.3 %collective-permute-done.2.refs_5_ = bf16[256,512]{1,0:T(8,128)(2,1)S(1)} collective-permute-done((bf16[256,512]{1,0:T(8,128)(2,1)S(1)}, bf16[256,512]{1,0:T(8,128)(2,1)S(1)}, u32[]{:S(2)}, u32[]{:S(2)}) %collective-permute-start.2) | collective-permute-done | bytes 262176 | tf_op jit(solution)/shard_map/ppermute | solution.py:42
  11.3 1.8 %collective-permute-start.3 = (bf16[256,512]{1,0:T(8,128)(2,1)S(1)}, bf16[256,512]{1,0:T(8,128)(2,1)S(1)}, u32[]{:S(2)}, u32[]{:S(2)}) collective-permute-start(bf16[256,512]{1,0:T(8,128)(2,1)S(1)} %collective-permute-done.2.refs_5_), channel_id=1, source_target_pairs={{0,2},{2,4},{4,6},{6,7},{7,5},{5,3},{3,1},{1,0},{8,10},{10,12},{12... | collective-permute-start | bytes 786440 | tf_op jit(solution)/shard_map/ppermute | solution.py:42
  13.3 5.5 %collective-permute-done.3.refs_7_ = bf16[256,512]{1,0:T(8,128)(2,1)S(1)} collective-permute-done((bf16[256,512]{1,0:T(8,128)(2,1)S(1)}, bf16[256,512]{1,0:T(8,128)(2,1)S(1)}, u32[]{:S(2)}, u32[]{:S(2)}) %collective-permute-start.3) | collective-permute-done | bytes 262176 | tf_op jit(solution)/shard_map/ppermute | solution.py:42
  18.8 1.5 %collective-permute-start.4 = (bf16[256,512]{1,0:T(8,128)(2,1)S(1)}, bf16[256,512]{1,0:T(8,128)(2,1)S(1)}, u32[]{:S(2)}, u32[]{:S(2)}) collective-permute-start(bf16[256,512]{1,0:T(8,128)(2,1)S(1)} %collective-permute-done.3.refs_7_), channel_id=1, source_target_pairs={{0,2},{2,4},{4,6},{6,7},{7,5},{5,3},{3,1},{1,0},{8,10},{10,12},{12... | collective-permute-start | bytes 786440 | tf_op jit(solution)/shard_map/ppermute | solution.py:42
  22.2 3.1 %collective-permute-done.4.refs_9_ = bf16[256,512]{1,0:T(8,128)(2,1)S(1)} collective-permute-done((bf16[256,512]{1,0:T(8,128)(2,1)S(1)}, bf16[256,512]{1,0:T(8,128)(2,1)S(1)}, u32[]{:S(2)}, u32[]{:S(2)}) %collective-permute-start.4) | collective-permute-done | bytes 262176 | tf_op jit(solution)/shard_map/ppermute | solution.py:42
  25.3 2.0 %collective-permute-done.7.refs_10_ = bf16[256,512]{1,0:T(8,128)(2,1)S(1)} collective-permute-done((bf16[256,512]{1,0:T(8,128)(2,1)S(1)}, bf16[256,512]{1,0:T(8,128)(2,1)S(1)}, u32[]{:S(2)}, u32[]{:S(2)}) %collective-permute-start.7) | collective-permute-done | bytes 262176 | tf_op jit(solution)/shard_map/ppermute | solution.py:42
  27.3 1.6 %collective-permute-start.9 = (bf16[256,512]{1,0:T(8,128)(2,1)S(1)}, bf16[256,512]{1,0:T(8,128)(2,1)S(1)}, u32[]{:S(2)}, u32[]{:S(2)}) collective-permute-start(bf16[256,512]{1,0:T(8,128)(2,1)S(1)} %broadcast_select_fusion), channel_id=1, source_target_pairs={{0,2},{2,4},{4,6},{6,7},{7,5},{5,3},{3,1},{1,0},{8,9},{10,8},{12,1... | collective-permute-start | bytes 786440 | tf_op jit(solution)/shard_map/ppermute | solution.py:51
  32.3 1.5 %collective-permute-done.9.refs_11_ = bf16[256,512]{1,0:T(8,128)(2,1)S(1)} collective-permute-done((bf16[256,512]{1,0:T(8,128)(2,1)S(1)}, bf16[256,512]{1,0:T(8,128)(2,1)S(1)}, u32[]{:S(2)}, u32[]{:S(2)}) %collective-permute-start.9) | collective-permute-done | bytes 262176 | tf_op jit(solution)/shard_map/ppermute | solution.py:51
  34.2 1.6 %collective-permute-start.11 = (bf16[128,384]{1,0:T(8,128)(2,1)S(1)}, bf16[128,384]{1,0:T(8,128)(2,1)S(1)}, u32[]{:S(2)}, u32[]{:S(2)}) collective-permute-start(bf16[128,384]{1,0:T(8,128)(2,1)S(1)} %get-tuple-element.43), channel_id=1, source_target_pairs={{0,16},{8,24},{16,0},{24,8},{1,17},{9,25},{17,1},{25,9},{2,18},{10... | collective-permute-start | bytes 294920 | tf_op jit(solution)/shard_map/ppermute | solution.py:330
  36.1 3.8 %collective-permute-done.11.refs_2_ = bf16[128,384]{1,0:T(8,128)(2,1)S(1)} collective-permute-done((bf16[128,384]{1,0:T(8,128)(2,1)S(1)}, bf16[128,384]{1,0:T(8,128)(2,1)S(1)}, u32[]{:S(2)}, u32[]{:S(2)}) %collective-permute-start.11) | collective-permute-done | bytes 98336 | tf_op jit(solution)/shard_map/ppermute | solution.py:330
  41.1 1.5 %collective-permute-start.20 = (bf16[512,512]{1,0:T(8,128)(2,1)S(1)}, bf16[512,512]{1,0:T(8,128)(2,1)S(1)}, u32[]{:S(2)}, u32[]{:S(2)}) collective-permute-start(bf16[512,512]{1,0:T(8,128)(2,1)S(1)} %get-tuple-element.48.refs_5_), channel_id=1, source_target_pairs={{0,16},{8,24},{16,0},{24,8},{1,17},{9,25},{17,1},{25,9},{2,18},{10... | collective-permute-start | bytes 1572872 | tf_op jit(solution)/shard_map/ppermute | solution.py:74
  42.8 1.6 %collective-permute-start.13 = (bf16[144,512]{1,0:T(8,128)(2,1)S(1)}, bf16[144,512]{1,0:T(8,128)(2,1)S(1)}, u32[]{:S(2)}, u32[]{:S(2)}) collective-permute-start(bf16[144,512]{1,0:T(8,128)(2,1)S(1)} %get-tuple-element.45.refs_0_.own), channel_id=1, source_target_pairs={{0,2},{2,4},{4,6},{6,7},{7,5},{5,3},{3,1},{1,0},{8,10},{10,12},{12... | collective-permute-start | bytes 442376 | tf_op jit(solution)/shard_map/ppermute | solution.py:42
  44.8 3.7 %collective-permute-done.13.refs_1_ = bf16[144,512]{1,0:T(8,128)(2,1)S(1)} collective-permute-done((bf16[144,512]{1,0:T(8,128)(2,1)S(1)}, bf16[144,512]{1,0:T(8,128)(2,1)S(1)}, u32[]{:S(2)}, u32[]{:S(2)}) %collective-permute-start.13) | collective-permute-done | bytes 147488 | tf_op jit(solution)/shard_map/ppermute | solution.py:42
  48.6 1.6 %collective-permute-start.14 = (bf16[144,512]{1,0:T(8,128)(2,1)S(1)}, bf16[144,512]{1,0:T(8,128)(2,1)S(1)}, u32[]{:S(2)}, u32[]{:S(2)}) collective-permute-start(bf16[144,512]{1,0:T(8,128)(2,1)S(1)} %collective-permute-done.13.refs_1_), channel_id=1, source_target_pairs={{0,2},{2,4},{4,6},{6,7},{7,5},{5,3},{3,1},{1,0},{8,10},{10,12},{12... | collective-permute-start | bytes 442376 | tf_op jit(solution)/shard_map/ppermute | solution.py:42
  50.6 3.1 %collective-permute-done.14.refs_3_ = bf16[144,512]{1,0:T(8,128)(2,1)S(1)} collective-permute-done((bf16[144,512]{1,0:T(8,128)(2,1)S(1)}, bf16[144,512]{1,0:T(8,128)(2,1)S(1)}, u32[]{:S(2)}, u32[]{:S(2)}) %collective-permute-start.14) | collective-permute-done | bytes 147488 | tf_op jit(solution)/shard_map/ppermute | solution.py:42
  53.7 1.6 %collective-permute-done.17.refs_4_ = bf16[144,512]{1,0:T(8,128)(2,1)S(1)} collective-permute-done((bf16[144,512]{1,0:T(8,128)(2,1)S(1)}, bf16[144,512]{1,0:T(8,128)(2,1)S(1)}, u32[]{:S(2)}, u32[]{:S(2)}) %collective-permute-start.17) | collective-permute-done | bytes 147488 | tf_op jit(solution)/shard_map/ppermute | solution.py:42
  55.3 1.6 %collective-permute-start.15 = (bf16[144,512]{1,0:T(8,128)(2,1)S(1)}, bf16[144,512]{1,0:T(8,128)(2,1)S(1)}, u32[]{:S(2)}, u32[]{:S(2)}) collective-permute-start(bf16[144,512]{1,0:T(8,128)(2,1)S(1)} %collective-permute-done.14.refs_3_), channel_id=1, source_target_pairs={{0,2},{2,4},{4,6},{6,7},{7,5},{5,3},{3,1},{1,0},{8,10},{10,12},{12... | collective-permute-start | bytes 442376 | tf_op jit(solution)/shard_map/ppermute | solution.py:42
  57.3 3.3 %attend_start.1 = (bf16[1024,512]{1,0:T(8,128)(2,1)S(1)}, bf16[512,1024]{1,0:T(8,128)(2,1)S(1)}, f32[1024,128]{1,0:T(8,128)S(1)}, f32[1024,128]{1,0:T(8,128)S(1)}, f32[1024,512]{1,0:T(8,128)S(1)}) custom-call(s32[1,3]{1,0:T(1,128)S(1)} %copy-done.7, bf16[128,1024]{1,0:T(8,128)(2,1)S(1)} %get-tuple-element.46.query, ...), custom_call_target="tpu_custom_call" | custom-call | flops 1342177280 | bytes 4194304 | tf_op jit(solution)/shard_map/attend_start/pallas_call | solution.py:357
  62.9 1.6 %collective-permute-start.22 = (bf16[144,512]{1,0:T(8,128)(2,1)S(1)}, bf16[144,512]{1,0:T(8,128)(2,1)S(1)}, u32[]{:S(2)}, u32[]{:S(2)}) collective-permute-start(bf16[144,512]{1,0:T(8,128)(2,1)S(1)} %broadcast_select_fusion.1), channel_id=1, source_target_pairs={{0,2},{2,4},{4,6},{6,7},{7,5},{5,3},{3,1},{1,0},{8,9},{10,8},{12,1... | collective-permute-start | bytes 442376 | tf_op jit(solution)/shard_map/ppermute | solution.py:51
  64.4 2.2 %attend_more.1 = (f32[1024,128]{1,0:T(8,128)S(1)}, f32[1024,128]{1,0:T(8,128)S(1)}, f32[1024,128]{1,0:T(8,128)S(1)}) custom-call(s32[1,3]{1,0:T(1,128)S(1)} %copy-done.7, bf16[144,512]{1,0:T(8,128)(2,1)S(1)} %get-tuple-element.45.refs_0_.own, bf16[1024,512]{1,0:T(8,128)(2,1)S(1)} %get-tuple-element.55.turned, bf16[512,1024]{1,0:T(8,128)(2,1)S(1)} %get-tuple-element.56.value, ...), custom_call_target="tpu_custom_call" | custom-call | flops 536870912 | bytes 4194304 | tf_op jit(solution)/shard_map/attend_more/pallas_call | solution.py:378
  66.6 1.4 %collective-permute-done.22.last = bf16[144,512]{1,0:T(8,128)(2,1)S(1)} collective-permute-done((bf16[144,512]{1,0:T(8,128)(2,1)S(1)}, bf16[144,512]{1,0:T(8,128)(2,1)S(1)}, u32[]{:S(2)}, u32[]{:S(2)}) %collective-permute-start.22) | collective-permute-done | bytes 147488 | tf_op jit(solution)/shard_map/ppermute | solution.py:51
  68.1 2.1 %attend.1 = bf16[128,1024]{1,0:T(8,128)(2,1)} custom-call(s32[1,3]{1,0:T(1,128)S(1)} %copy-done.7, bf16[144,512]{1,0:T(8,128)(2,1)S(1)} %get-tuple-element.45.refs_0_.own, bf16[1024,512]{1,0:T(8,128)(2,1)S(1)} %get-tuple-element.55.turned, bf16[512,1024]{1,0:T(8,128)(2,1)S(1)} %get-tuple-element.56.value, f32[1024,128]{1,0:T(8,128)S(1)} %get-tuple-element.60.peaks, ...), custom_call_target="tpu_custom_call" | custom-call | flops 536870912 | bytes 4194304 | tf_op jit(solution)/shard_map/attend/pallas_call | solution.py:391
  (50 shorter events, 15.0 us)
Async XLA Ops:
  1.9 9.3 %collective-permute-start.2 = (bf16[256,512]{1,0:T(8,128)(2,1)S(1)}, bf16[256,512]{1,0:T(8,128)(2,1)S(1)}, u32[]{:S(2)}, u32[]{:S(2)}) collective-permute-start(bf16[256,512]{1,0:T(8,128)(2,1)S(1)} %pack.1.refs_4_), channel_id=1, source_target_pairs={{0,2},{2,4},{4,6},{6,7},{7,5},{5,3},{3,1},{1,0},{8,10},{10,12},{12... | collective-permute-start | bytes 786440 | tf_op jit(solution)/shard_map/ppermute | solution.py:42
  5.0 8.0 %collective-permute-start.5 = (bf16[256,512]{1,0:T(8,128)(2,1)S(1)}, bf16[256,512]{1,0:T(8,128)(2,1)S(1)}, u32[]{:S(2)}, u32[]{:S(2)}) collective-permute-start(bf16[256,512]{1,0:T(8,128)(2,1)S(1)} %pack.1.refs_4_), channel_id=1, source_target_pairs={{0,1},{2,0},{4,2},{6,4},{7,6},{5,7},{3,5},{1,3},{8,9},{10,8},{12,1... | collective-permute-start | bytes 786440 | tf_op jit(solution)/shard_map/ppermute | solution.py:42
  6.9 15.3 %collective-permute-start.1 = (bf16[128,2048]{1,0:T(8,128)(2,1)S(1)}, bf16[128,2048]{1,0:T(8,128)(2,1)S(1)}, u32[]{:S(2)}, u32[]{:S(2)}) collective-permute-start(bf16[128,2048]{1,0:T(8,128)(2,1)S(1)} %get-tuple-element.37.refs_0_), channel_id=1, source_target_pairs={{0,16},{8,24},{16,0},{24,8},{1,17},{9,25},{17,1},{25,9},{2,18},{10... | collective-permute-start | bytes 1572872 | tf_op jit(solution)/shard_map/ppermute | solution.py:74
  11.3 7.5 %collective-permute-start.3 = (bf16[256,512]{1,0:T(8,128)(2,1)S(1)}, bf16[256,512]{1,0:T(8,128)(2,1)S(1)}, u32[]{:S(2)}, u32[]{:S(2)}) collective-permute-start(bf16[256,512]{1,0:T(8,128)(2,1)S(1)} %collective-permute-done.2.refs_5_), channel_id=1, source_target_pairs={{0,2},{2,4},{4,6},{6,7},{7,5},{5,3},{3,1},{1,0},{8,10},{10,12},{12... | collective-permute-start | bytes 786440 | tf_op jit(solution)/shard_map/ppermute | solution.py:42
  13.1 7.9 %collective-permute-start.6 = (bf16[256,512]{1,0:T(8,128)(2,1)S(1)}, bf16[256,512]{1,0:T(8,128)(2,1)S(1)}, u32[]{:S(2)}, u32[]{:S(2)}) collective-permute-start(bf16[256,512]{1,0:T(8,128)(2,1)S(1)} %collective-permute-done.5.refs_6_), channel_id=1, source_target_pairs={{0,1},{2,0},{4,2},{6,4},{7,6},{5,7},{3,5},{1,3},{8,9},{10,8},{12,1... | collective-permute-start | bytes 786440 | tf_op jit(solution)/shard_map/ppermute | solution.py:42
  18.8 6.6 %collective-permute-start.4 = (bf16[256,512]{1,0:T(8,128)(2,1)S(1)}, bf16[256,512]{1,0:T(8,128)(2,1)S(1)}, u32[]{:S(2)}, u32[]{:S(2)}) collective-permute-start(bf16[256,512]{1,0:T(8,128)(2,1)S(1)} %collective-permute-done.3.refs_7_), channel_id=1, source_target_pairs={{0,2},{2,4},{4,6},{6,7},{7,5},{5,3},{3,1},{1,0},{8,10},{10,12},{12... | collective-permute-start | bytes 786440 | tf_op jit(solution)/shard_map/ppermute | solution.py:42
  20.9 6.4 %collective-permute-start.7 = (bf16[256,512]{1,0:T(8,128)(2,1)S(1)}, bf16[256,512]{1,0:T(8,128)(2,1)S(1)}, u32[]{:S(2)}, u32[]{:S(2)}) collective-permute-start(bf16[256,512]{1,0:T(8,128)(2,1)S(1)} %collective-permute-done.6.refs_8_), channel_id=1, source_target_pairs={{0,1},{2,0},{4,2},{6,4},{7,6},{5,7},{3,5},{1,3},{8,9},{10,8},{12,1... | collective-permute-start | bytes 786440 | tf_op jit(solution)/shard_map/ppermute | solution.py:42
  22.2 6.8 %collective-permute-start = (bf16[128,2048]{1,0:T(8,128)(2,1)S(1)}, bf16[128,2048]{1,0:T(8,128)(2,1)S(1)}, u32[]{:S(2)}, u32[]{:S(2)}) collective-permute-start(bf16[128,2048]{1,0:T(8,128)(2,1)S(1)} %get-tuple-element.37.refs_0_), channel_id=1, source_target_pairs={{0,8},{8,0},{16,24},{24,16},{1,9},{9,1},{17,25},{25,17},{2,10},{10... | collective-permute-start | bytes 1572872 | tf_op jit(solution)/shard_map/ppermute | solution.py:74
  27.3 1.9 %collective-permute-start.8 = (bf16[128,2048]{1,0:T(8,128)(2,1)S(1)}, bf16[128,2048]{1,0:T(8,128)(2,1)S(1)}, u32[]{:S(2)}, u32[]{:S(2)}) collective-permute-start(bf16[128,2048]{1,0:T(8,128)(2,1)S(1)} %collective-permute-done.1.refs_2_), channel_id=1, source_target_pairs={{0,8},{8,0},{16,24},{24,16},{1,9},{9,1},{17,25},{25,17},{2,10},{10... | collective-permute-start | bytes 1572872 | tf_op jit(solution)/shard_map/ppermute | solution.py:74
  27.3 6.4 %collective-permute-start.9 = (bf16[256,512]{1,0:T(8,128)(2,1)S(1)}, bf16[256,512]{1,0:T(8,128)(2,1)S(1)}, u32[]{:S(2)}, u32[]{:S(2)}) collective-permute-start(bf16[256,512]{1,0:T(8,128)(2,1)S(1)} %broadcast_select_fusion), channel_id=1, source_target_pairs={{0,2},{2,4},{4,6},{6,7},{7,5},{5,3},{3,1},{1,0},{8,9},{10,8},{12,1... | collective-permute-start | bytes 786440 | tf_op jit(solution)/shard_map/ppermute | solution.py:51
  32.2 25.1 %copy-start.7 = (s32[1,3]{1,0:T(1,128)S(1)}, s32[1,3]{1,0:T(1,128)}, u32[]{:S(2)}) copy-start(s32[1,3]{1,0:T(1,128)} %lengths.5) | copy-start | bytes 40
  34.1 1.9 %collective-permute-start.10 = (bf16[128,384]{1,0:T(8,128)(2,1)S(1)}, bf16[128,384]{1,0:T(8,128)(2,1)S(1)}, u32[]{:S(2)}, u32[]{:S(2)}) collective-permute-start(bf16[128,384]{1,0:T(8,128)(2,1)S(1)} %get-tuple-element.42), channel_id=1, source_target_pairs={{0,8},{8,0},{16,24},{24,16},{1,9},{9,1},{17,25},{25,17},{2,10},{10... | collective-permute-start | bytes 294920 | tf_op jit(solution)/shard_map/ppermute | solution.py:330
  34.2 5.7 %collective-permute-start.11 = (bf16[128,384]{1,0:T(8,128)(2,1)S(1)}, bf16[128,384]{1,0:T(8,128)(2,1)S(1)}, u32[]{:S(2)}, u32[]{:S(2)}) collective-permute-start(bf16[128,384]{1,0:T(8,128)(2,1)S(1)} %get-tuple-element.43), channel_id=1, source_target_pairs={{0,16},{8,24},{16,0},{24,8},{1,17},{9,25},{17,1},{25,9},{2,18},{10... | collective-permute-start | bytes 294920 | tf_op jit(solution)/shard_map/ppermute | solution.py:330
  35.8 5.3 %collective-permute-start.12 = (bf16[128,384]{1,0:T(8,128)(2,1)S(1)}, bf16[128,384]{1,0:T(8,128)(2,1)S(1)}, u32[]{:S(2)}, u32[]{:S(2)}) collective-permute-start(bf16[128,384]{1,0:T(8,128)(2,1)S(1)} %get-tuple-element.44), channel_id=1, source_target_pairs={{0,24},{8,16},{16,8},{24,0},{1,25},{9,17},{17,9},{25,1},{2,26},{10... | collective-permute-start | bytes 294920 | tf_op jit(solution)/shard_map/ppermute | solution.py:330
  41.1 14.2 %collective-permute-start.20 = (bf16[512,512]{1,0:T(8,128)(2,1)S(1)}, bf16[512,512]{1,0:T(8,128)(2,1)S(1)}, u32[]{:S(2)}, u32[]{:S(2)}) collective-permute-start(bf16[512,512]{1,0:T(8,128)(2,1)S(1)} %get-tuple-element.48.refs_5_), channel_id=1, source_target_pairs={{0,16},{8,24},{16,0},{24,8},{1,17},{9,25},{17,1},{25,9},{2,18},{10... | collective-permute-start | bytes 1572872 | tf_op jit(solution)/shard_map/ppermute | solution.py:74
  42.8 5.8 %collective-permute-start.13 = (bf16[144,512]{1,0:T(8,128)(2,1)S(1)}, bf16[144,512]{1,0:T(8,128)(2,1)S(1)}, u32[]{:S(2)}, u32[]{:S(2)}) collective-permute-start(bf16[144,512]{1,0:T(8,128)(2,1)S(1)} %get-tuple-element.45.refs_0_.own), channel_id=1, source_target_pairs={{0,2},{2,4},{4,6},{6,7},{7,5},{5,3},{3,1},{1,0},{8,10},{10,12},{12... | collective-permute-start | bytes 442376 | tf_op jit(solution)/shard_map/ppermute | solution.py:42
  44.4 5.8 %collective-permute-start.16 = (bf16[144,512]{1,0:T(8,128)(2,1)S(1)}, bf16[144,512]{1,0:T(8,128)(2,1)S(1)}, u32[]{:S(2)}, u32[]{:S(2)}) collective-permute-start(bf16[144,512]{1,0:T(8,128)(2,1)S(1)} %get-tuple-element.45.refs_0_.own), channel_id=1, source_target_pairs={{0,1},{2,0},{4,2},{6,4},{7,6},{5,7},{3,5},{1,3},{8,9},{10,8},{12,1... | collective-permute-start | bytes 442376 | tf_op jit(solution)/shard_map/ppermute | solution.py:42
  48.6 5.1 %collective-permute-start.14 = (bf16[144,512]{1,0:T(8,128)(2,1)S(1)}, bf16[144,512]{1,0:T(8,128)(2,1)S(1)}, u32[]{:S(2)}, u32[]{:S(2)}) collective-permute-start(bf16[144,512]{1,0:T(8,128)(2,1)S(1)} %collective-permute-done.13.refs_1_), channel_id=1, source_target_pairs={{0,2},{2,4},{4,6},{6,7},{7,5},{5,3},{3,1},{1,0},{8,10},{10,12},{12... | collective-permute-start | bytes 442376 | tf_op jit(solution)/shard_map/ppermute | solution.py:42
  50.1 5.1 %collective-permute-start.17 = (bf16[144,512]{1,0:T(8,128)(2,1)S(1)}, bf16[144,512]{1,0:T(8,128)(2,1)S(1)}, u32[]{:S(2)}, u32[]{:S(2)}) collective-permute-start(bf16[144,512]{1,0:T(8,128)(2,1)S(1)} %collective-permute-done.16.refs_2_), channel_id=1, source_target_pairs={{0,1},{2,0},{4,2},{6,4},{7,6},{5,7},{3,5},{1,3},{8,9},{10,8},{12,1... | collective-permute-start | bytes 442376 | tf_op jit(solution)/shard_map/ppermute | solution.py:42
  50.6 6.7 %collective-permute-start.19 = (bf16[512,512]{1,0:T(8,128)(2,1)S(1)}, bf16[512,512]{1,0:T(8,128)(2,1)S(1)}, u32[]{:S(2)}, u32[]{:S(2)}) collective-permute-start(bf16[512,512]{1,0:T(8,128)(2,1)S(1)} %get-tuple-element.48.refs_5_), channel_id=1, source_target_pairs={{0,8},{8,0},{16,24},{24,16},{1,9},{9,1},{17,25},{25,17},{2,10},{10... | collective-permute-start | bytes 1572872 | tf_op jit(solution)/shard_map/ppermute | solution.py:74
  55.3 2.0 %collective-permute-start.21 = (bf16[512,512]{1,0:T(8,128)(2,1)S(1)}, bf16[512,512]{1,0:T(8,128)(2,1)S(1)}, u32[]{:S(2)}, u32[]{:S(2)}) collective-permute-start(bf16[512,512]{1,0:T(8,128)(2,1)S(1)} %collective-permute-done.20.refs_7_), channel_id=1, source_target_pairs={{0,8},{8,0},{16,24},{24,16},{1,9},{9,1},{17,25},{25,17},{2,10},{10... | collective-permute-start | bytes 1572872 | tf_op jit(solution)/shard_map/ppermute | solution.py:74
  55.3 6.3 %collective-permute-start.15 = (bf16[144,512]{1,0:T(8,128)(2,1)S(1)}, bf16[144,512]{1,0:T(8,128)(2,1)S(1)}, u32[]{:S(2)}, u32[]{:S(2)}) collective-permute-start(bf16[144,512]{1,0:T(8,128)(2,1)S(1)} %collective-permute-done.14.refs_3_), channel_id=1, source_target_pairs={{0,2},{2,4},{4,6},{6,7},{7,5},{5,3},{3,1},{1,0},{8,10},{10,12},{12... | collective-permute-start | bytes 442376 | tf_op jit(solution)/shard_map/ppermute | solution.py:42
  56.9 6.0 %collective-permute-start.18 = (bf16[144,512]{1,0:T(8,128)(2,1)S(1)}, bf16[144,512]{1,0:T(8,128)(2,1)S(1)}, u32[]{:S(2)}, u32[]{:S(2)}) collective-permute-start(bf16[144,512]{1,0:T(8,128)(2,1)S(1)} %collective-permute-done.17.refs_4_), channel_id=1, source_target_pairs={{0,1},{2,0},{4,2},{6,4},{7,6},{5,7},{3,5},{1,3},{8,9},{10,8},{12,1... | collective-permute-start | bytes 442376 | tf_op jit(solution)/shard_map/ppermute | solution.py:42
  62.9 5.2 %collective-permute-start.22 = (bf16[144,512]{1,0:T(8,128)(2,1)S(1)}, bf16[144,512]{1,0:T(8,128)(2,1)S(1)}, u32[]{:S(2)}, u32[]{:S(2)}) collective-permute-start(bf16[144,512]{1,0:T(8,128)(2,1)S(1)} %broadcast_select_fusion.1), channel_id=1, source_target_pairs={{0,2},{2,4},{4,6},{6,7},{7,5},{5,3},{3,1},{1,0},{8,9},{10,8},{12,1... | collective-permute-start | bytes 442376 | tf_op jit(solution)/shard_map/ppermute | solution.py:51
  (8 other events, 6.9 us)

commit v2 on v0

--- a/solution.py
+++ b/solution.py
@@ -197,7 +197,7 @@
 
 
 def start_kernel(count, size, lengths, query, *refs):
-    blocks, refs = refs[: count - 3], refs[count - 3 :]
+    blocks, refs = refs[: count - 5], refs[count - 5 :]
     expands, refs = refs[:size], refs[size:]
     turned, value, peaks, sums, summed, latent, expand, scores, probs = refs
     rows = query.shape[0]
@@ -360,7 +360,7 @@
         compiler_params=grant(16),
         name="assemble",
     )(digits, *back)
-    total, early = count * rows, count - 3
+    total, early = count * rows, count - 5
     needed = grant(8 + total * HEADS * rows * 8 // (1024 * 1024))
     state = [jax.ShapeDtypeStruct((HEADS * rows, width), jnp.float32) for width in (HDIM, HDIM, rank)]
 
@@ -397,14 +397,14 @@
     running = pl.pallas_call(
         more_kernel,
         out_shape=[jax.ShapeDtypeStruct((HEADS * rows, HDIM), jnp.float32)] * 3,
-        in_specs=[SMEM] + [VMEM] * 8,
+        in_specs=[SMEM] + [VMEM] * 10,
         out_specs=[VMEM] * 3,
         scratch_shapes=[
-            pltpu.VMEM((2 * rows, rank), jnp.bfloat16),
-            pltpu.VMEM((HEADS * rows, 2 * rows), jnp.float32),
+            pltpu.VMEM((4 * rows, rank), jnp.bfloat16),
+            pltpu.VMEM((HEADS * rows, 4 * rows), jnp.float32),
         ],
         compiler_params=grant(16),
-        cost_estimate=cost(2),
+        cost_estimate=cost(4),
         name="attend_more",
     )(lengths, block, turned, value, *running, *lat_blocks[early : count - 1])
     return pl.pallas_call(

time: 69.8 us -> 69.8 us (level)
    pallas_call x1, Pallas kernels: 3.35 us -> 2.53 us  [attend_start(): pl.pallas_call(functools.partial(start_kernel, count, size), out_shape=[j...]
    ppermute x3, waiting for transfers between devices: 7.7 us -> 8.51 us  [split_ring_gather(): lax.ppermute(below, 'mp', up)]
  transfers between devices with their start and end apart: 24 -> 24, of which waited for: 14 -> 14; matrix products, arithmetic and copies ran while one was open for 0% -> 0% of each run, Pallas kernels for 10% -> 9%
where the time goes in v2:
time: 69.8 us; the launch traced here: 69.5 us
  waiting for transfers between devices  34.4 us (49%)
  starting transfers between devices  22.4 us (32%)
  Pallas kernels  9.07 us (13%)
  local copies, waits for them, and re-layouts  3.62 us (5%)
    ppermute x3, waiting for transfers between devices, ring_gather(): lax.ppermute(below, 'mp', up)  12.3 us
    ppermute x3, waiting for transfers between devices, split_ring_gather(): lax.ppermute(below, 'mp', up)  8.51 us
    ppermute x3, starting transfers between devices, ring_gather(): lax.ppermute(below, 'mp', up)  6.35 us
    ppermute x3, waiting for transfers between devices, body(): lax.ppermute(projs[k], 'group', [(i, i ^ k) for i in range(size)])  5 us
    ppermute x3, starting transfers between devices, split_ring_gather(): lax.ppermute(below, 'mp', up)  4.78 us
    unnamed x10, local copies, waits for them, and re-layouts  3.6 us
    ppermute x6, starting transfers between devices, group_gather(): blocks[k ^ bit] = lax.ppermute(sent, 'group', pairs)  3.41 us
    ppermute x1, waiting for transfers between devices, ring_gather(): lax.ppermute(above[cut:], 'mp', down)  2.95 us
  transfers between devices with their start and end apart: 24, of which 14 were waited for; matrix products, arithmetic and copies ran while one was open for 0% of the time, Pallas kernels for 9%

profile of v2, /device:TPU:0, one launch (start us, length us, event | category | flops | bytes accessed | tf_op | source)
XLA Modules:
  0.0 69.5 jit_solution(692121954010130840)
XLA Ops:
  1.9 3.1 %collective-permute-start.2 = (bf16[256,512]{1,0:T(8,128)(2,1)S(1)}, bf16[256,512]{1,0:T(8,128)(2,1)S(1)}, u32[]{:S(2)}, u32[]{:S(2)}) collective-permute-start(bf16[256,512]{1,0:T(8,128)(2,1)S(1)} %pack.1.refs_4_), channel_id=1, source_target_pairs={{0,2},{2,4},{4,6},{6,7},{7,5},{5,3},{3,1},{1,0},{8,10},{10,12},{12... | collective-permute-start | bytes 786440 | tf_op jit(solution)/shard_map/ppermute | solution.py:42
  6.9 2.0 %collective-permute-start.1 = (bf16[128,2048]{1,0:T(8,128)(2,1)S(1)}, bf16[128,2048]{1,0:T(8,128)(2,1)S(1)}, u32[]{:S(2)}, u32[]{:S(2)}) collective-permute-start(bf16[128,2048]{1,0:T(8,128)(2,1)S(1)} %get-tuple-element.35.refs_0_), channel_id=1, source_target_pairs={{0,16},{8,24},{16,0},{24,8},{1,17},{9,25},{17,1},{25,9},{2,18},{10... | collective-permute-start | bytes 1572872 | tf_op jit(solution)/shard_map/ppermute | solution.py:91
  8.9 2.3 %collective-permute-done.2.refs_5_ = bf16[256,512]{1,0:T(8,128)(2,1)S(1)} collective-permute-done((bf16[256,512]{1,0:T(8,128)(2,1)S(1)}, bf16[256,512]{1,0:T(8,128)(2,1)S(1)}, u32[]{:S(2)}, u32[]{:S(2)}) %collective-permute-start.2) | collective-permute-done | bytes 262176 | tf_op jit(solution)/shard_map/ppermute | solution.py:42
  11.3 1.8 %collective-permute-start.3 = (bf16[256,512]{1,0:T(8,128)(2,1)S(1)}, bf16[256,512]{1,0:T(8,128)(2,1)S(1)}, u32[]{:S(2)}, u32[]{:S(2)}) collective-permute-start(bf16[256,512]{1,0:T(8,128)(2,1)S(1)} %collective-permute-done.2.refs_5_), channel_id=1, source_target_pairs={{0,2},{2,4},{4,6},{6,7},{7,5},{5,3},{3,1},{1,0},{8,10},{10,12},{12... | collective-permute-start | bytes 786440 | tf_op jit(solution)/shard_map/ppermute | solution.py:42
  13.3 5.5 %collective-permute-done.3.refs_7_ = bf16[256,512]{1,0:T(8,128)(2,1)S(1)} collective-permute-done((bf16[256,512]{1,0:T(8,128)(2,1)S(1)}, bf16[256,512]{1,0:T(8,128)(2,1)S(1)}, u32[]{:S(2)}, u32[]{:S(2)}) %collective-permute-start.3) | collective-permute-done | bytes 262176 | tf_op jit(solution)/shard_map/ppermute | solution.py:42
  18.8 1.5 %collective-permute-start.4 = (bf16[256,512]{1,0:T(8,128)(2,1)S(1)}, bf16[256,512]{1,0:T(8,128)(2,1)S(1)}, u32[]{:S(2)}, u32[]{:S(2)}) collective-permute-start(bf16[256,512]{1,0:T(8,128)(2,1)S(1)} %collective-permute-done.3.refs_7_), channel_id=1, source_target_pairs={{0,2},{2,4},{4,6},{6,7},{7,5},{5,3},{3,1},{1,0},{8,10},{10,12},{12... | collective-permute-start | bytes 786440 | tf_op jit(solution)/shard_map/ppermute | solution.py:42
  20.8 4.5 %collective-permute-done.4.refs_9_ = bf16[256,512]{1,0:T(8,128)(2,1)S(1)} collective-permute-done((bf16[256,512]{1,0:T(8,128)(2,1)S(1)}, bf16[256,512]{1,0:T(8,128)(2,1)S(1)}, u32[]{:S(2)}, u32[]{:S(2)}) %collective-permute-start.4) | collective-permute-done | bytes 262176 | tf_op jit(solution)/shard_map/ppermute | solution.py:42
  27.2 1.5 %collective-permute-start.9 = (bf16[128,512]{1,0:T(8,128)(2,1)S(1)}, bf16[128,512]{1,0:T(8,128)(2,1)S(1)}, u32[]{:S(2)}, u32[]{:S(2)}) collective-permute-start(bf16[128,512]{1,0:T(8,128)(2,1)S(1)} %slice.8), channel_id=1, source_target_pairs={{0,2},{2,4},{4,6},{6,7},{7,5},{5,3},{3,1},{1,0},{8,10},{10,12},{12... | collective-permute-start | bytes 393224 | tf_op jit(solution)/shard_map/ppermute | solution.py:45
  29.6 2.9 %collective-permute-done.10.refs_12_ = bf16[128,512]{1,0:T(8,128)(2,1)S(1)} collective-permute-done((bf16[128,512]{1,0:T(8,128)(2,1)S(1)}, bf16[128,512]{1,0:T(8,128)(2,1)S(1)}, u32[]{:S(2)}, u32[]{:S(2)}) %collective-permute-start.10) | collective-permute-done | bytes 131104 | tf_op jit(solution)/shard_map/ppermute | solution.py:45
  33.7 1.5 %collective-permute-start.12 = (bf16[128,384]{1,0:T(8,128)(2,1)S(1)}, bf16[128,384]{1,0:T(8,128)(2,1)S(1)}, u32[]{:S(2)}, u32[]{:S(2)}) collective-permute-start(bf16[128,384]{1,0:T(8,128)(2,1)S(1)} %get-tuple-element.39), channel_id=1, source_target_pairs={{0,16},{8,24},{16,0},{24,8},{1,17},{9,25},{17,1},{25,9},{2,18},{10... | collective-permute-start | bytes 294920 | tf_op jit(solution)/shard_map/ppermute | solution.py:349
  35.6 3.8 %collective-permute-done.12.refs_2_ = bf16[128,384]{1,0:T(8,128)(2,1)S(1)} collective-permute-done((bf16[128,384]{1,0:T(8,128)(2,1)S(1)}, bf16[128,384]{1,0:T(8,128)(2,1)S(1)}, u32[]{:S(2)}, u32[]{:S(2)}) %collective-permute-start.12) | collective-permute-done | bytes 98336 | tf_op jit(solution)/shard_map/ppermute | solution.py:349
  40.6 1.4 %collective-permute-start.21 = (bf16[512,512]{1,0:T(8,128)(2,1)S(1)}, bf16[512,512]{1,0:T(8,128)(2,1)S(1)}, u32[]{:S(2)}, u32[]{:S(2)}) collective-permute-start(bf16[512,512]{1,0:T(8,128)(2,1)S(1)} %get-tuple-element.44.refs_3_), channel_id=1, source_target_pairs={{0,16},{8,24},{16,0},{24,8},{1,17},{9,25},{17,1},{25,9},{2,18},{10... | collective-permute-start | bytes 1572872 | tf_op jit(solution)/shard_map/ppermute | solution.py:91
  42.2 1.6 %collective-permute-start.14 = (bf16[144,512]{1,0:T(8,128)(2,1)S(1)}, bf16[144,512]{1,0:T(8,128)(2,1)S(1)}, u32[]{:S(2)}, u32[]{:S(2)}) collective-permute-start(bf16[144,512]{1,0:T(8,128)(2,1)S(1)} %get-tuple-element.41.refs_0_.own), channel_id=1, source_target_pairs={{0,2},{2,4},{4,6},{6,7},{7,5},{5,3},{3,1},{1,0},{8,10},{10,12},{12... | collective-permute-start | bytes 442376 | tf_op jit(solution)/shard_map/ppermute | solution.py:53
  44.2 3.7 %collective-permute-done.14.refs_1_ = bf16[144,512]{1,0:T(8,128)(2,1)S(1)} collective-permute-done((bf16[144,512]{1,0:T(8,128)(2,1)S(1)}, bf16[144,512]{1,0:T(8,128)(2,1)S(1)}, u32[]{:S(2)}, u32[]{:S(2)}) %collective-permute-start.14) | collective-permute-done | bytes 147488 | tf_op jit(solution)/shard_map/ppermute | solution.py:53
  48.0 1.6 %collective-permute-start.15 = (bf16[144,512]{1,0:T(8,128)(2,1)S(1)}, bf16[144,512]{1,0:T(8,128)(2,1)S(1)}, u32[]{:S(2)}, u32[]{:S(2)}) collective-permute-start(bf16[144,512]{1,0:T(8,128)(2,1)S(1)} %collective-permute-done.14.refs_1_), channel_id=1, source_target_pairs={{0,2},{2,4},{4,6},{6,7},{7,5},{5,3},{3,1},{1,0},{8,10},{10,12},{12... | collective-permute-start | bytes 442376 | tf_op jit(solution)/shard_map/ppermute | solution.py:53
  50.0 3.1 %collective-permute-done.15.refs_0_ = bf16[144,512]{1,0:T(8,128)(2,1)S(1)} collective-permute-done((bf16[144,512]{1,0:T(8,128)(2,1)S(1)}, bf16[144,512]{1,0:T(8,128)(2,1)S(1)}, u32[]{:S(2)}, u32[]{:S(2)}) %collective-permute-start.15) | collective-permute-done | bytes 147488 | tf_op jit(solution)/shard_map/ppermute | solution.py:53
  53.1 1.6 %collective-permute-done.18.refs_1_ = bf16[144,512]{1,0:T(8,128)(2,1)S(1)} collective-permute-done((bf16[144,512]{1,0:T(8,128)(2,1)S(1)}, bf16[144,512]{1,0:T(8,128)(2,1)S(1)}, u32[]{:S(2)}, u32[]{:S(2)}) %collective-permute-start.18) | collective-permute-done | bytes 147488 | tf_op jit(solution)/shard_map/ppermute | solution.py:53
  54.7 1.6 %collective-permute-start.16 = (bf16[144,512]{1,0:T(8,128)(2,1)S(1)}, bf16[144,512]{1,0:T(8,128)(2,1)S(1)}, u32[]{:S(2)}, u32[]{:S(2)}) collective-permute-start(bf16[144,512]{1,0:T(8,128)(2,1)S(1)} %collective-permute-done.15.refs_0_), channel_id=1, source_target_pairs={{0,2},{2,4},{4,6},{6,7},{7,5},{5,3},{3,1},{1,0},{8,10},{10,12},{12... | collective-permute-start | bytes 442376 | tf_op jit(solution)/shard_map/ppermute | solution.py:53
  56.7 2.5 %attend_start.1 = (bf16[1024,512]{1,0:T(8,128)(2,1)S(1)}, bf16[512,1024]{1,0:T(8,128)(2,1)S(1)}, f32[1024,128]{1,0:T(8,128)S(1)}, f32[1024,128]{1,0:T(8,128)S(1)}, f32[1024,512]{1,0:T(8,128)S(1)}) custom-call(s32[1,3]{1,0:T(1,128)S(1)} %copy-done.3, bf16[128,1024]{1,0:T(8,128)(2,1)S(1)} %get-tuple-element.42.query, ...), custom_call_target="tpu_custom_call" | custom-call | flops 805306368 | bytes 4194304 | tf_op jit(solution)/shard_map/attend_start/pallas_call | solution.py:376
  59.3 1.7 %collective-permute-done.16.refs_2_ = bf16[144,512]{1,0:T(8,128)(2,1)S(1)} collective-permute-done((bf16[144,512]{1,0:T(8,128)(2,1)S(1)}, bf16[144,512]{1,0:T(8,128)(2,1)S(1)}, u32[]{:S(2)}, u32[]{:S(2)}) %collective-permute-start.16) | collective-permute-done | bytes 147488 | tf_op jit(solution)/shard_map/ppermute | solution.py:53
  61.0 1.3 %collective-permute-done.19.refs_3_ = bf16[144,512]{1,0:T(8,128)(2,1)S(1)} collective-permute-done((bf16[144,512]{1,0:T(8,128)(2,1)S(1)}, bf16[144,512]{1,0:T(8,128)(2,1)S(1)}, u32[]{:S(2)}, u32[]{:S(2)}) %collective-permute-start.19) | collective-permute-done | bytes 147488 | tf_op jit(solution)/shard_map/ppermute | solution.py:53
  62.3 1.6 %collective-permute-start.23 = (bf16[144,512]{1,0:T(8,128)(2,1)S(1)}, bf16[144,512]{1,0:T(8,128)(2,1)S(1)}, u32[]{:S(2)}, u32[]{:S(2)}) collective-permute-start(bf16[144,512]{1,0:T(8,128)(2,1)S(1)} %broadcast_select_fusion), channel_id=1, source_target_pairs={{0,2},{2,4},{4,6},{6,7},{7,5},{5,3},{3,1},{1,0},{8,9},{10,8},{12,1... | collective-permute-start | bytes 442376 | tf_op jit(solution)/shard_map/ppermute | solution.py:63
  63.9 2.5 %attend_more.1 = (f32[1024,128]{1,0:T(8,128)S(1)}, f32[1024,128]{1,0:T(8,128)S(1)}, f32[1024,128]{1,0:T(8,128)S(1)}) custom-call(s32[1,3]{1,0:T(1,128)S(1)} %copy-done.3, bf16[144,512]{1,0:T(8,128)(2,1)S(1)} %get-tuple-element.41.refs_0_.own, bf16[1024,512]{1,0:T(8,128)(2,1)S(1)} %get-tuple-element.51.turned, bf16[512,1024]{1,0:T(8,128)(2,1)S(1)} %get-tuple-element.52.value, ...), custom_call_target="tpu_custom_call" | custom-call | flops 1073741824 | bytes 4194304 | tf_op jit(solution)/shard_map/attend_more/pallas_call | solution.py:397
  67.5 2.1 %attend.1 = bf16[128,1024]{1,0:T(8,128)(2,1)} custom-call(s32[1,3]{1,0:T(1,128)S(1)} %copy-done.3, bf16[144,512]{1,0:T(8,128)(2,1)S(1)} %get-tuple-element.41.refs_0_.own, bf16[1024,512]{1,0:T(8,128)(2,1)S(1)} %get-tuple-element.51.turned, bf16[512,1024]{1,0:T(8,128)(2,1)S(1)} %get-tuple-element.52.value, f32[1024,128]{1,0:T(8,128)S(1)} %get-tuple-element.56.peaks, ...), custom_call_target="tpu_custom_call" | custom-call | flops 536870912 | bytes 4194304 | tf_op jit(solution)/shard_map/attend/pallas_call | solution.py:410
  (45 shorter events, 12.7 us)
Async XLA Ops:
  1.9 9.3 %collective-permute-start.2 = (bf16[256,512]{1,0:T(8,128)(2,1)S(1)}, bf16[256,512]{1,0:T(8,128)(2,1)S(1)}, u32[]{:S(2)}, u32[]{:S(2)}) collective-permute-start(bf16[256,512]{1,0:T(8,128)(2,1)S(1)} %pack.1.refs_4_), channel_id=1, source_target_pairs={{0,2},{2,4},{4,6},{6,7},{7,5},{5,3},{3,1},{1,0},{8,10},{10,12},{12... | collective-permute-start | bytes 786440 | tf_op jit(solution)/shard_map/ppermute | solution.py:42
  5.0 8.0 %collective-permute-start.5 = (bf16[256,512]{1,0:T(8,128)(2,1)S(1)}, bf16[256,512]{1,0:T(8,128)(2,1)S(1)}, u32[]{:S(2)}, u32[]{:S(2)}) collective-permute-start(bf16[256,512]{1,0:T(8,128)(2,1)S(1)} %pack.1.refs_4_), channel_id=1, source_target_pairs={{0,1},{2,0},{4,2},{6,4},{7,6},{5,7},{3,5},{1,3},{8,9},{10,8},{12,1... | collective-permute-start | bytes 786440 | tf_op jit(solution)/shard_map/ppermute | solution.py:42
  6.9 13.9 %collective-permute-start.1 = (bf16[128,2048]{1,0:T(8,128)(2,1)S(1)}, bf16[128,2048]{1,0:T(8,128)(2,1)S(1)}, u32[]{:S(2)}, u32[]{:S(2)}) collective-permute-start(bf16[128,2048]{1,0:T(8,128)(2,1)S(1)} %get-tuple-element.35.refs_0_), channel_id=1, source_target_pairs={{0,16},{8,24},{16,0},{24,8},{1,17},{9,25},{17,1},{25,9},{2,18},{10... | collective-permute-start | bytes 1572872 | tf_op jit(solution)/shard_map/ppermute | solution.py:91
  11.3 7.5 %collective-permute-start.3 = (bf16[256,512]{1,0:T(8,128)(2,1)S(1)}, bf16[256,512]{1,0:T(8,128)(2,1)S(1)}, u32[]{:S(2)}, u32[]{:S(2)}) collective-permute-start(bf16[256,512]{1,0:T(8,128)(2,1)S(1)} %collective-permute-done.2.refs_5_), channel_id=1, source_target_pairs={{0,2},{2,4},{4,6},{6,7},{7,5},{5,3},{3,1},{1,0},{8,10},{10,12},{12... | collective-permute-start | bytes 786440 | tf_op jit(solution)/shard_map/ppermute | solution.py:42
  13.1 7.2 %collective-permute-start.6 = (bf16[256,512]{1,0:T(8,128)(2,1)S(1)}, bf16[256,512]{1,0:T(8,128)(2,1)S(1)}, u32[]{:S(2)}, u32[]{:S(2)}) collective-permute-start(bf16[256,512]{1,0:T(8,128)(2,1)S(1)} %collective-permute-done.5.refs_6_), channel_id=1, source_target_pairs={{0,1},{2,0},{4,2},{6,4},{7,6},{5,7},{3,5},{1,3},{8,9},{10,8},{12,1... | collective-permute-start | bytes 786440 | tf_op jit(solution)/shard_map/ppermute | solution.py:42
  18.8 6.6 %collective-permute-start.4 = (bf16[256,512]{1,0:T(8,128)(2,1)S(1)}, bf16[256,512]{1,0:T(8,128)(2,1)S(1)}, u32[]{:S(2)}, u32[]{:S(2)}) collective-permute-start(bf16[256,512]{1,0:T(8,128)(2,1)S(1)} %collective-permute-done.3.refs_7_), channel_id=1, source_target_pairs={{0,2},{2,4},{4,6},{6,7},{7,5},{5,3},{3,1},{1,0},{8,10},{10,12},{12... | collective-permute-start | bytes 786440 | tf_op jit(solution)/shard_map/ppermute | solution.py:42
  20.2 6.4 %collective-permute-start.7 = (bf16[256,512]{1,0:T(8,128)(2,1)S(1)}, bf16[256,512]{1,0:T(8,128)(2,1)S(1)}, u32[]{:S(2)}, u32[]{:S(2)}) collective-permute-start(bf16[256,512]{1,0:T(8,128)(2,1)S(1)} %collective-permute-done.6.refs_8_), channel_id=1, source_target_pairs={{0,1},{2,0},{4,2},{6,4},{7,6},{5,7},{3,5},{1,3},{8,9},{10,8},{12,1... | collective-permute-start | bytes 786440 | tf_op jit(solution)/shard_map/ppermute | solution.py:42
  20.8 8.0 %collective-permute-start = (bf16[128,2048]{1,0:T(8,128)(2,1)S(1)}, bf16[128,2048]{1,0:T(8,128)(2,1)S(1)}, u32[]{:S(2)}, u32[]{:S(2)}) collective-permute-start(bf16[128,2048]{1,0:T(8,128)(2,1)S(1)} %get-tuple-element.35.refs_0_), channel_id=1, source_target_pairs={{0,8},{8,0},{16,24},{24,16},{1,9},{9,1},{17,25},{25,17},{2,10},{10... | collective-permute-start | bytes 1572872 | tf_op jit(solution)/shard_map/ppermute | solution.py:91
  26.6 2.2 %collective-permute-start.8 = (bf16[128,2048]{1,0:T(8,128)(2,1)S(1)}, bf16[128,2048]{1,0:T(8,128)(2,1)S(1)}, u32[]{:S(2)}, u32[]{:S(2)}) collective-permute-start(bf16[128,2048]{1,0:T(8,128)(2,1)S(1)} %collective-permute-done.1.refs_2_), channel_id=1, source_target_pairs={{0,8},{8,0},{16,24},{24,16},{1,9},{9,1},{17,25},{25,17},{2,10},{10... | collective-permute-start | bytes 1572872 | tf_op jit(solution)/shard_map/ppermute | solution.py:91
  26.6 6.0 %collective-permute-start.10 = (bf16[128,512]{1,0:T(8,128)(2,1)S(1)}, bf16[128,512]{1,0:T(8,128)(2,1)S(1)}, u32[]{:S(2)}, u32[]{:S(2)}) collective-permute-start(bf16[128,512]{1,0:T(8,128)(2,1)S(1)} %slice.9), channel_id=1, source_target_pairs={{0,1},{2,0},{4,2},{6,4},{7,6},{5,7},{3,5},{1,3},{8,9},{10,8},{12,1... | collective-permute-start | bytes 393224 | tf_op jit(solution)/shard_map/ppermute | solution.py:45
  27.2 5.7 %collective-permute-start.9 = (bf16[128,512]{1,0:T(8,128)(2,1)S(1)}, bf16[128,512]{1,0:T(8,128)(2,1)S(1)}, u32[]{:S(2)}, u32[]{:S(2)}) collective-permute-start(bf16[128,512]{1,0:T(8,128)(2,1)S(1)} %slice.8), channel_id=1, source_target_pairs={{0,2},{2,4},{4,6},{6,7},{7,5},{5,3},{3,1},{1,0},{8,10},{10,12},{12... | collective-permute-start | bytes 393224 | tf_op jit(solution)/shard_map/ppermute | solution.py:45
  33.6 1.9 %collective-permute-start.11 = (bf16[128,384]{1,0:T(8,128)(2,1)S(1)}, bf16[128,384]{1,0:T(8,128)(2,1)S(1)}, u32[]{:S(2)}, u32[]{:S(2)}) collective-permute-start(bf16[128,384]{1,0:T(8,128)(2,1)S(1)} %get-tuple-element.38), channel_id=1, source_target_pairs={{0,8},{8,0},{16,24},{24,16},{1,9},{9,1},{17,25},{25,17},{2,10},{10... | collective-permute-start | bytes 294920 | tf_op jit(solution)/shard_map/ppermute | solution.py:349
  33.7 5.7 %collective-permute-start.12 = (bf16[128,384]{1,0:T(8,128)(2,1)S(1)}, bf16[128,384]{1,0:T(8,128)(2,1)S(1)}, u32[]{:S(2)}, u32[]{:S(2)}) collective-permute-start(bf16[128,384]{1,0:T(8,128)(2,1)S(1)} %get-tuple-element.39), channel_id=1, source_target_pairs={{0,16},{8,24},{16,0},{24,8},{1,17},{9,25},{17,1},{25,9},{2,18},{10... | collective-permute-start | bytes 294920 | tf_op jit(solution)/shard_map/ppermute | solution.py:349
  35.2 5.4 %collective-permute-start.13 = (bf16[128,384]{1,0:T(8,128)(2,1)S(1)}, bf16[128,384]{1,0:T(8,128)(2,1)S(1)}, u32[]{:S(2)}, u32[]{:S(2)}) collective-permute-start(bf16[128,384]{1,0:T(8,128)(2,1)S(1)} %get-tuple-element.40), channel_id=1, source_target_pairs={{0,24},{8,16},{16,8},{24,0},{1,25},{9,17},{17,9},{25,1},{2,26},{10... | collective-permute-start | bytes 294920 | tf_op jit(solution)/shard_map/ppermute | solution.py:349
  40.6 14.1 %collective-permute-start.21 = (bf16[512,512]{1,0:T(8,128)(2,1)S(1)}, bf16[512,512]{1,0:T(8,128)(2,1)S(1)}, u32[]{:S(2)}, u32[]{:S(2)}) collective-permute-start(bf16[512,512]{1,0:T(8,128)(2,1)S(1)} %get-tuple-element.44.refs_3_), channel_id=1, source_target_pairs={{0,16},{8,24},{16,0},{24,8},{1,17},{9,25},{17,1},{25,9},{2,18},{10... | collective-permute-start | bytes 1572872 | tf_op jit(solution)/shard_map/ppermute | solution.py:91
  42.2 5.8 %collective-permute-start.14 = (bf16[144,512]{1,0:T(8,128)(2,1)S(1)}, bf16[144,512]{1,0:T(8,128)(2,1)S(1)}, u32[]{:S(2)}, u32[]{:S(2)}) collective-permute-start(bf16[144,512]{1,0:T(8,128)(2,1)S(1)} %get-tuple-element.41.refs_0_.own), channel_id=1, source_target_pairs={{0,2},{2,4},{4,6},{6,7},{7,5},{5,3},{3,1},{1,0},{8,10},{10,12},{12... | collective-permute-start | bytes 442376 | tf_op jit(solution)/shard_map/ppermute | solution.py:53
  43.8 5.8 %collective-permute-start.17 = (bf16[144,512]{1,0:T(8,128)(2,1)S(1)}, bf16[144,512]{1,0:T(8,128)(2,1)S(1)}, u32[]{:S(2)}, u32[]{:S(2)}) collective-permute-start(bf16[144,512]{1,0:T(8,128)(2,1)S(1)} %get-tuple-element.41.refs_0_.own), channel_id=1, source_target_pairs={{0,1},{2,0},{4,2},{6,4},{7,6},{5,7},{3,5},{1,3},{8,9},{10,8},{12,1... | collective-permute-start | bytes 442376 | tf_op jit(solution)/shard_map/ppermute | solution.py:53
  48.0 5.1 %collective-permute-start.15 = (bf16[144,512]{1,0:T(8,128)(2,1)S(1)}, bf16[144,512]{1,0:T(8,128)(2,1)S(1)}, u32[]{:S(2)}, u32[]{:S(2)}) collective-permute-start(bf16[144,512]{1,0:T(8,128)(2,1)S(1)} %collective-permute-done.14.refs_1_), channel_id=1, source_target_pairs={{0,2},{2,4},{4,6},{6,7},{7,5},{5,3},{3,1},{1,0},{8,10},{10,12},{12... | collective-permute-start | bytes 442376 | tf_op jit(solution)/shard_map/ppermute | solution.py:53
  49.5 5.1 %collective-permute-start.18 = (bf16[144,512]{1,0:T(8,128)(2,1)S(1)}, bf16[144,512]{1,0:T(8,128)(2,1)S(1)}, u32[]{:S(2)}, u32[]{:S(2)}) collective-permute-start(bf16[144,512]{1,0:T(8,128)(2,1)S(1)} %collective-permute-done.17.refs_2_), channel_id=1, source_target_pairs={{0,1},{2,0},{4,2},{6,4},{7,6},{5,7},{3,5},{1,3},{8,9},{10,8},{12,1... | collective-permute-start | bytes 442376 | tf_op jit(solution)/shard_map/ppermute | solution.py:53
  50.0 6.7 %collective-permute-start.20 = (bf16[512,512]{1,0:T(8,128)(2,1)S(1)}, bf16[512,512]{1,0:T(8,128)(2,1)S(1)}, u32[]{:S(2)}, u32[]{:S(2)}) collective-permute-start(bf16[512,512]{1,0:T(8,128)(2,1)S(1)} %get-tuple-element.44.refs_3_), channel_id=1, source_target_pairs={{0,8},{8,0},{16,24},{24,16},{1,9},{9,1},{17,25},{25,17},{2,10},{10... | collective-permute-start | bytes 1572872 | tf_op jit(solution)/shard_map/ppermute | solution.py:91
  54.7 2.0 %collective-permute-start.22 = (bf16[512,512]{1,0:T(8,128)(2,1)S(1)}, bf16[512,512]{1,0:T(8,128)(2,1)S(1)}, u32[]{:S(2)}, u32[]{:S(2)}) collective-permute-start(bf16[512,512]{1,0:T(8,128)(2,1)S(1)} %collective-permute-done.21.refs_5_), channel_id=1, source_target_pairs={{0,8},{8,0},{16,24},{24,16},{1,9},{9,1},{17,25},{25,17},{2,10},{10... | collective-permute-start | bytes 1572872 | tf_op jit(solution)/shard_map/ppermute | solution.py:91
  54.7 6.3 %collective-permute-start.16 = (bf16[144,512]{1,0:T(8,128)(2,1)S(1)}, bf16[144,512]{1,0:T(8,128)(2,1)S(1)}, u32[]{:S(2)}, u32[]{:S(2)}) collective-permute-start(bf16[144,512]{1,0:T(8,128)(2,1)S(1)} %collective-permute-done.15.refs_0_), channel_id=1, source_target_pairs={{0,2},{2,4},{4,6},{6,7},{7,5},{5,3},{3,1},{1,0},{8,10},{10,12},{12... | collective-permute-start | bytes 442376 | tf_op jit(solution)/shard_map/ppermute | solution.py:53
  56.3 6.0 %collective-permute-start.19 = (bf16[144,512]{1,0:T(8,128)(2,1)S(1)}, bf16[144,512]{1,0:T(8,128)(2,1)S(1)}, u32[]{:S(2)}, u32[]{:S(2)}) collective-permute-start(bf16[144,512]{1,0:T(8,128)(2,1)S(1)} %collective-permute-done.18.refs_1_), channel_id=1, source_target_pairs={{0,1},{2,0},{4,2},{6,4},{7,6},{5,7},{3,5},{1,3},{8,9},{10,8},{12,1... | collective-permute-start | bytes 442376 | tf_op jit(solution)/shard_map/ppermute | solution.py:53
  62.3 5.2 %collective-permute-start.23 = (bf16[144,512]{1,0:T(8,128)(2,1)S(1)}, bf16[144,512]{1,0:T(8,128)(2,1)S(1)}, u32[]{:S(2)}, u32[]{:S(2)}) collective-permute-start(bf16[144,512]{1,0:T(8,128)(2,1)S(1)} %broadcast_select_fusion), channel_id=1, source_target_pairs={{0,2},{2,4},{4,6},{6,7},{7,5},{5,3},{3,1},{1,0},{8,9},{10,8},{12,1... | collective-permute-start | bytes 442376 | tf_op jit(solution)/shard_map/ppermute | solution.py:63
  (5 other events, 30.7 us)

commit v3 on v0

--- a/solution.py
+++ b/solution.py
@@ -314,7 +314,7 @@
         name="norm",
     )(arrivals, slots.reshape(1, rows))
     tokens = group_gather(normed, size, blocks[-4:-2])
-    early = 0 if w_joined.shape[0] // 2 % 128 else count - 3
+    early = 0 if w_joined.shape[0] // 2 % 128 else count - 1
     total = []
     if early:
         total = [

time: 69.8 us -> 69.5 us (level)
  no operation moved by 1% of the time
where the time goes in v3:
time: 69.5 us; the launch traced here: 69.3 us
  waiting for transfers between devices  33.6 us (48%)
  starting transfers between devices  22.4 us (32%)
  Pallas kernels  9.57 us (14%)
  local copies, waits for them, and re-layouts  3.62 us (5%)
    ppermute x3, waiting for transfers between devices, ring_gather(): lax.ppermute(below, 'mp', up)  12.3 us
    ppermute x3, waiting for transfers between devices, split_ring_gather(): lax.ppermute(below, 'mp', up)  7.69 us
    ppermute x3, starting transfers between devices, ring_gather(): lax.ppermute(below, 'mp', up)  6.35 us
    ppermute x3, waiting for transfers between devices, body(): lax.ppermute(projs[k], 'group', [(i, i ^ k) for i in range(size)])  5 us
    ppermute x3, starting transfers between devices, split_ring_gather(): lax.ppermute(below, 'mp', up)  4.78 us
    unnamed x10, local copies, waits for them, and re-layouts  3.6 us
    ppermute x6, starting transfers between devices, group_gather(): blocks[k ^ bit] = lax.ppermute(sent, 'group', pairs)  3.4 us
    pallas_call x1, Pallas kernels, attend_start(): pl.pallas_call(functools.partial(start_kernel, count, size), out_shape=[j...  3.36 us
  transfers between devices with their start and end apart: 24, of which 14 were waited for; matrix products, arithmetic and copies ran while one was open for 0% of the time, Pallas kernels for 10%

profile of v3, /device:TPU:0, one launch (start us, length us, event | category | flops | bytes accessed | tf_op | source)
XLA Modules:
  0.0 69.3 jit_solution(5111700029940907133)
XLA Ops:
  1.9 3.1 %collective-permute-start.2 = (bf16[256,512]{1,0:T(8,128)(2,1)S(1)}, bf16[256,512]{1,0:T(8,128)(2,1)S(1)}, u32[]{:S(2)}, u32[]{:S(2)}) collective-permute-start(bf16[256,512]{1,0:T(8,128)(2,1)S(1)} %pack.1.refs_4_), channel_id=1, source_target_pairs={{0,2},{2,4},{4,6},{6,7},{7,5},{5,3},{3,1},{1,0},{8,10},{10,12},{12... | collective-permute-start | bytes 786440 | tf_op jit(solution)/shard_map/ppermute | solution.py:42
  6.9 2.0 %collective-permute-start.1 = (bf16[128,2048]{1,0:T(8,128)(2,1)S(1)}, bf16[128,2048]{1,0:T(8,128)(2,1)S(1)}, u32[]{:S(2)}, u32[]{:S(2)}) collective-permute-start(bf16[128,2048]{1,0:T(8,128)(2,1)S(1)} %get-tuple-element.35.refs_0_), channel_id=1, source_target_pairs={{0,16},{8,24},{16,0},{24,8},{1,17},{9,25},{17,1},{25,9},{2,18},{10... | collective-permute-start | bytes 1572872 | tf_op jit(solution)/shard_map/ppermute | solution.py:91
  8.9 2.3 %collective-permute-done.2.refs_5_ = bf16[256,512]{1,0:T(8,128)(2,1)S(1)} collective-permute-done((bf16[256,512]{1,0:T(8,128)(2,1)S(1)}, bf16[256,512]{1,0:T(8,128)(2,1)S(1)}, u32[]{:S(2)}, u32[]{:S(2)}) %collective-permute-start.2) | collective-permute-done | bytes 262176 | tf_op jit(solution)/shard_map/ppermute | solution.py:42
  11.3 1.8 %collective-permute-start.3 = (bf16[256,512]{1,0:T(8,128)(2,1)S(1)}, bf16[256,512]{1,0:T(8,128)(2,1)S(1)}, u32[]{:S(2)}, u32[]{:S(2)}) collective-permute-start(bf16[256,512]{1,0:T(8,128)(2,1)S(1)} %collective-permute-done.2.refs_5_), channel_id=1, source_target_pairs={{0,2},{2,4},{4,6},{6,7},{7,5},{5,3},{3,1},{1,0},{8,10},{10,12},{12... | collective-permute-start | bytes 786440 | tf_op jit(solution)/shard_map/ppermute | solution.py:42
  13.3 5.5 %collective-permute-done.3.refs_7_ = bf16[256,512]{1,0:T(8,128)(2,1)S(1)} collective-permute-done((bf16[256,512]{1,0:T(8,128)(2,1)S(1)}, bf16[256,512]{1,0:T(8,128)(2,1)S(1)}, u32[]{:S(2)}, u32[]{:S(2)}) %collective-permute-start.3) | collective-permute-done | bytes 262176 | tf_op jit(solution)/shard_map/ppermute | solution.py:42
  18.8 1.5 %collective-permute-start.4 = (bf16[256,512]{1,0:T(8,128)(2,1)S(1)}, bf16[256,512]{1,0:T(8,128)(2,1)S(1)}, u32[]{:S(2)}, u32[]{:S(2)}) collective-permute-start(bf16[256,512]{1,0:T(8,128)(2,1)S(1)} %collective-permute-done.3.refs_7_), channel_id=1, source_target_pairs={{0,2},{2,4},{4,6},{6,7},{7,5},{5,3},{3,1},{1,0},{8,10},{10,12},{12... | collective-permute-start | bytes 786440 | tf_op jit(solution)/shard_map/ppermute | solution.py:42
  20.8 4.5 %collective-permute-done.4.refs_9_ = bf16[256,512]{1,0:T(8,128)(2,1)S(1)} collective-permute-done((bf16[256,512]{1,0:T(8,128)(2,1)S(1)}, bf16[256,512]{1,0:T(8,128)(2,1)S(1)}, u32[]{:S(2)}, u32[]{:S(2)}) %collective-permute-start.4) | collective-permute-done | bytes 262176 | tf_op jit(solution)/shard_map/ppermute | solution.py:42
  27.2 1.5 %collective-permute-start.9 = (bf16[128,512]{1,0:T(8,128)(2,1)S(1)}, bf16[128,512]{1,0:T(8,128)(2,1)S(1)}, u32[]{:S(2)}, u32[]{:S(2)}) collective-permute-start(bf16[128,512]{1,0:T(8,128)(2,1)S(1)} %slice.8), channel_id=1, source_target_pairs={{0,2},{2,4},{4,6},{6,7},{7,5},{5,3},{3,1},{1,0},{8,10},{10,12},{12... | collective-permute-start | bytes 393224 | tf_op jit(solution)/shard_map/ppermute | solution.py:45
  29.9 2.7 %collective-permute-done.10.refs_12_ = bf16[128,512]{1,0:T(8,128)(2,1)S(1)} collective-permute-done((bf16[128,512]{1,0:T(8,128)(2,1)S(1)}, bf16[128,512]{1,0:T(8,128)(2,1)S(1)}, u32[]{:S(2)}, u32[]{:S(2)}) %collective-permute-start.10) | collective-permute-done | bytes 131104 | tf_op jit(solution)/shard_map/ppermute | solution.py:45
  33.4 1.5 %collective-permute-start.12 = (bf16[128,384]{1,0:T(8,128)(2,1)S(1)}, bf16[128,384]{1,0:T(8,128)(2,1)S(1)}, u32[]{:S(2)}, u32[]{:S(2)}) collective-permute-start(bf16[128,384]{1,0:T(8,128)(2,1)S(1)} %get-tuple-element.39), channel_id=1, source_target_pairs={{0,16},{8,24},{16,0},{24,8},{1,17},{9,25},{17,1},{25,9},{2,18},{10... | collective-permute-start | bytes 294920 | tf_op jit(solution)/shard_map/ppermute | solution.py:349
  35.3 3.8 %collective-permute-done.12.refs_2_ = bf16[128,384]{1,0:T(8,128)(2,1)S(1)} collective-permute-done((bf16[128,384]{1,0:T(8,128)(2,1)S(1)}, bf16[128,384]{1,0:T(8,128)(2,1)S(1)}, u32[]{:S(2)}, u32[]{:S(2)}) %collective-permute-start.12) | collective-permute-done | bytes 98336 | tf_op jit(solution)/shard_map/ppermute | solution.py:349
  40.3 1.4 %collective-permute-start.21 = (bf16[512,512]{1,0:T(8,128)(2,1)S(1)}, bf16[512,512]{1,0:T(8,128)(2,1)S(1)}, u32[]{:S(2)}, u32[]{:S(2)}) collective-permute-start(bf16[512,512]{1,0:T(8,128)(2,1)S(1)} %get-tuple-element.44.refs_5_), channel_id=1, source_target_pairs={{0,16},{8,24},{16,0},{24,8},{1,17},{9,25},{17,1},{25,9},{2,18},{10... | collective-permute-start | bytes 1572872 | tf_op jit(solution)/shard_map/ppermute | solution.py:91
  41.9 1.6 %collective-permute-start.14 = (bf16[144,512]{1,0:T(8,128)(2,1)S(1)}, bf16[144,512]{1,0:T(8,128)(2,1)S(1)}, u32[]{:S(2)}, u32[]{:S(2)}) collective-permute-start(bf16[144,512]{1,0:T(8,128)(2,1)S(1)} %get-tuple-element.41.refs_0_.own), channel_id=1, source_target_pairs={{0,2},{2,4},{4,6},{6,7},{7,5},{5,3},{3,1},{1,0},{8,10},{10,12},{12... | collective-permute-start | bytes 442376 | tf_op jit(solution)/shard_map/ppermute | solution.py:53
  44.0 3.7 %collective-permute-done.14.refs_1_ = bf16[144,512]{1,0:T(8,128)(2,1)S(1)} collective-permute-done((bf16[144,512]{1,0:T(8,128)(2,1)S(1)}, bf16[144,512]{1,0:T(8,128)(2,1)S(1)}, u32[]{:S(2)}, u32[]{:S(2)}) %collective-permute-start.14) | collective-permute-done | bytes 147488 | tf_op jit(solution)/shard_map/ppermute | solution.py:53
  47.7 1.6 %collective-permute-start.15 = (bf16[144,512]{1,0:T(8,128)(2,1)S(1)}, bf16[144,512]{1,0:T(8,128)(2,1)S(1)}, u32[]{:S(2)}, u32[]{:S(2)}) collective-permute-start(bf16[144,512]{1,0:T(8,128)(2,1)S(1)} %collective-permute-done.14.refs_1_), channel_id=1, source_target_pairs={{0,2},{2,4},{4,6},{6,7},{7,5},{5,3},{3,1},{1,0},{8,10},{10,12},{12... | collective-permute-start | bytes 442376 | tf_op jit(solution)/shard_map/ppermute | solution.py:53
  49.7 3.1 %collective-permute-done.15.refs_3_ = bf16[144,512]{1,0:T(8,128)(2,1)S(1)} collective-permute-done((bf16[144,512]{1,0:T(8,128)(2,1)S(1)}, bf16[144,512]{1,0:T(8,128)(2,1)S(1)}, u32[]{:S(2)}, u32[]{:S(2)}) %collective-permute-start.15) | collective-permute-done | bytes 147488 | tf_op jit(solution)/shard_map/ppermute | solution.py:53
  52.8 1.6 %collective-permute-done.18.refs_4_ = bf16[144,512]{1,0:T(8,128)(2,1)S(1)} collective-permute-done((bf16[144,512]{1,0:T(8,128)(2,1)S(1)}, bf16[144,512]{1,0:T(8,128)(2,1)S(1)}, u32[]{:S(2)}, u32[]{:S(2)}) %collective-permute-start.18) | collective-permute-done | bytes 147488 | tf_op jit(solution)/shard_map/ppermute | solution.py:53
  54.4 1.6 %collective-permute-start.16 = (bf16[144,512]{1,0:T(8,128)(2,1)S(1)}, bf16[144,512]{1,0:T(8,128)(2,1)S(1)}, u32[]{:S(2)}, u32[]{:S(2)}) collective-permute-start(bf16[144,512]{1,0:T(8,128)(2,1)S(1)} %collective-permute-done.15.refs_3_), channel_id=1, source_target_pairs={{0,2},{2,4},{4,6},{6,7},{7,5},{5,3},{3,1},{1,0},{8,10},{10,12},{12... | collective-permute-start | bytes 442376 | tf_op jit(solution)/shard_map/ppermute | solution.py:53
  56.5 3.4 %attend_start.1 = (bf16[1024,512]{1,0:T(8,128)(2,1)S(1)}, bf16[512,1024]{1,0:T(8,128)(2,1)S(1)}, f32[1024,128]{1,0:T(8,128)S(1)}, f32[1024,128]{1,0:T(8,128)S(1)}, f32[1024,512]{1,0:T(8,128)S(1)}) custom-call(s32[1,3]{1,0:T(1,128)S(1)} %copy-done.3, bf16[128,1024]{1,0:T(8,128)(2,1)S(1)} %get-tuple-element.42.query, ...), custom_call_target="tpu_custom_call" | custom-call | flops 1342177280 | bytes 4194304 | tf_op jit(solution)/shard_map/attend_start/pallas_call | solution.py:376
  60.7 1.3 %collective-permute-done.19.refs_1_ = bf16[144,512]{1,0:T(8,128)(2,1)S(1)} collective-permute-done((bf16[144,512]{1,0:T(8,128)(2,1)S(1)}, bf16[144,512]{1,0:T(8,128)(2,1)S(1)}, u32[]{:S(2)}, u32[]{:S(2)}) %collective-permute-start.19) | collective-permute-done | bytes 147488 | tf_op jit(solution)/shard_map/ppermute | solution.py:53
  62.0 1.6 %collective-permute-start.23 = (bf16[144,512]{1,0:T(8,128)(2,1)S(1)}, bf16[144,512]{1,0:T(8,128)(2,1)S(1)}, u32[]{:S(2)}, u32[]{:S(2)}) collective-permute-start(bf16[144,512]{1,0:T(8,128)(2,1)S(1)} %broadcast_select_fusion), channel_id=1, source_target_pairs={{0,2},{2,4},{4,6},{6,7},{7,5},{5,3},{3,1},{1,0},{8,9},{10,8},{12,1... | collective-permute-start | bytes 442376 | tf_op jit(solution)/shard_map/ppermute | solution.py:63
  63.6 2.2 %attend_more.1 = (f32[1024,128]{1,0:T(8,128)S(1)}, f32[1024,128]{1,0:T(8,128)S(1)}, f32[1024,128]{1,0:T(8,128)S(1)}) custom-call(s32[1,3]{1,0:T(1,128)S(1)} %copy-done.3, bf16[144,512]{1,0:T(8,128)(2,1)S(1)} %get-tuple-element.41.refs_0_.own, bf16[1024,512]{1,0:T(8,128)(2,1)S(1)} %get-tuple-element.51.turned, bf16[512,1024]{1,0:T(8,128)(2,1)S(1)} %get-tuple-element.52.value, ...), custom_call_target="tpu_custom_call" | custom-call | flops 536870912 | bytes 4194304 | tf_op jit(solution)/shard_map/attend_more/pallas_call | solution.py:397
  65.8 1.4 %collective-permute-done.23.last = bf16[144,512]{1,0:T(8,128)(2,1)S(1)} collective-permute-done((bf16[144,512]{1,0:T(8,128)(2,1)S(1)}, bf16[144,512]{1,0:T(8,128)(2,1)S(1)}, u32[]{:S(2)}, u32[]{:S(2)}) %collective-permute-start.23) | collective-permute-done | bytes 147488 | tf_op jit(solution)/shard_map/ppermute | solution.py:63
  67.2 2.1 %attend.1 = bf16[128,1024]{1,0:T(8,128)(2,1)} custom-call(s32[1,3]{1,0:T(1,128)S(1)} %copy-done.3, bf16[144,512]{1,0:T(8,128)(2,1)S(1)} %get-tuple-element.41.refs_0_.own, bf16[1024,512]{1,0:T(8,128)(2,1)S(1)} %get-tuple-element.51.turned, bf16[512,1024]{1,0:T(8,128)(2,1)S(1)} %get-tuple-element.52.value, f32[1024,128]{1,0:T(8,128)S(1)} %get-tuple-element.56.peaks, ...), custom_call_target="tpu_custom_call" | custom-call | flops 536870912 | bytes 4194304 | tf_op jit(solution)/shard_map/attend/pallas_call | solution.py:410
  (45 shorter events, 12.5 us)
Async XLA Ops:
  1.9 9.3 %collective-permute-start.2 = (bf16[256,512]{1,0:T(8,128)(2,1)S(1)}, bf16[256,512]{1,0:T(8,128)(2,1)S(1)}, u32[]{:S(2)}, u32[]{:S(2)}) collective-permute-start(bf16[256,512]{1,0:T(8,128)(2,1)S(1)} %pack.1.refs_4_), channel_id=1, source_target_pairs={{0,2},{2,4},{4,6},{6,7},{7,5},{5,3},{3,1},{1,0},{8,10},{10,12},{12... | collective-permute-start | bytes 786440 | tf_op jit(solution)/shard_map/ppermute | solution.py:42
  5.0 8.0 %collective-permute-start.5 = (bf16[256,512]{1,0:T(8,128)(2,1)S(1)}, bf16[256,512]{1,0:T(8,128)(2,1)S(1)}, u32[]{:S(2)}, u32[]{:S(2)}) collective-permute-start(bf16[256,512]{1,0:T(8,128)(2,1)S(1)} %pack.1.refs_4_), channel_id=1, source_target_pairs={{0,1},{2,0},{4,2},{6,4},{7,6},{5,7},{3,5},{1,3},{8,9},{10,8},{12,1... | collective-permute-start | bytes 786440 | tf_op jit(solution)/shard_map/ppermute | solution.py:42
  6.9 13.9 %collective-permute-start.1 = (bf16[128,2048]{1,0:T(8,128)(2,1)S(1)}, bf16[128,2048]{1,0:T(8,128)(2,1)S(1)}, u32[]{:S(2)}, u32[]{:S(2)}) collective-permute-start(bf16[128,2048]{1,0:T(8,128)(2,1)S(1)} %get-tuple-element.35.refs_0_), channel_id=1, source_target_pairs={{0,16},{8,24},{16,0},{24,8},{1,17},{9,25},{17,1},{25,9},{2,18},{10... | collective-permute-start | bytes 1572872 | tf_op jit(solution)/shard_map/ppermute | solution.py:91
  11.3 7.5 %collective-permute-start.3 = (bf16[256,512]{1,0:T(8,128)(2,1)S(1)}, bf16[256,512]{1,0:T(8,128)(2,1)S(1)}, u32[]{:S(2)}, u32[]{:S(2)}) collective-permute-start(bf16[256,512]{1,0:T(8,128)(2,1)S(1)} %collective-permute-done.2.refs_5_), channel_id=1, source_target_pairs={{0,2},{2,4},{4,6},{6,7},{7,5},{5,3},{3,1},{1,0},{8,10},{10,12},{12... | collective-permute-start | bytes 786440 | tf_op jit(solution)/shard_map/ppermute | solution.py:42
  13.1 7.2 %collective-permute-start.6 = (bf16[256,512]{1,0:T(8,128)(2,1)S(1)}, bf16[256,512]{1,0:T(8,128)(2,1)S(1)}, u32[]{:S(2)}, u32[]{:S(2)}) collective-permute-start(bf16[256,512]{1,0:T(8,128)(2,1)S(1)} %collective-permute-done.5.refs_6_), channel_id=1, source_target_pairs={{0,1},{2,0},{4,2},{6,4},{7,6},{5,7},{3,5},{1,3},{8,9},{10,8},{12,1... | collective-permute-start | bytes 786440 | tf_op jit(solution)/shard_map/ppermute | solution.py:42
  18.8 6.6 %collective-permute-start.4 = (bf16[256,512]{1,0:T(8,128)(2,1)S(1)}, bf16[256,512]{1,0:T(8,128)(2,1)S(1)}, u32[]{:S(2)}, u32[]{:S(2)}) collective-permute-start(bf16[256,512]{1,0:T(8,128)(2,1)S(1)} %collective-permute-done.3.refs_7_), channel_id=1, source_target_pairs={{0,2},{2,4},{4,6},{6,7},{7,5},{5,3},{3,1},{1,0},{8,10},{10,12},{12... | collective-permute-start | bytes 786440 | tf_op jit(solution)/shard_map/ppermute | solution.py:42
  20.2 6.4 %collective-permute-start.7 = (bf16[256,512]{1,0:T(8,128)(2,1)S(1)}, bf16[256,512]{1,0:T(8,128)(2,1)S(1)}, u32[]{:S(2)}, u32[]{:S(2)}) collective-permute-start(bf16[256,512]{1,0:T(8,128)(2,1)S(1)} %collective-permute-done.6.refs_8_), channel_id=1, source_target_pairs={{0,1},{2,0},{4,2},{6,4},{7,6},{5,7},{3,5},{1,3},{8,9},{10,8},{12,1... | collective-permute-start | bytes 786440 | tf_op jit(solution)/shard_map/ppermute | solution.py:42
  20.8 8.0 %collective-permute-start = (bf16[128,2048]{1,0:T(8,128)(2,1)S(1)}, bf16[128,2048]{1,0:T(8,128)(2,1)S(1)}, u32[]{:S(2)}, u32[]{:S(2)}) collective-permute-start(bf16[128,2048]{1,0:T(8,128)(2,1)S(1)} %get-tuple-element.35.refs_0_), channel_id=1, source_target_pairs={{0,8},{8,0},{16,24},{24,16},{1,9},{9,1},{17,25},{25,17},{2,10},{10... | collective-permute-start | bytes 1572872 | tf_op jit(solution)/shard_map/ppermute | solution.py:91
  26.6 2.2 %collective-permute-start.8 = (bf16[128,2048]{1,0:T(8,128)(2,1)S(1)}, bf16[128,2048]{1,0:T(8,128)(2,1)S(1)}, u32[]{:S(2)}, u32[]{:S(2)}) collective-permute-start(bf16[128,2048]{1,0:T(8,128)(2,1)S(1)} %collective-permute-done.1.refs_2_), channel_id=1, source_target_pairs={{0,8},{8,0},{16,24},{24,16},{1,9},{9,1},{17,25},{25,17},{2,10},{10... | collective-permute-start | bytes 1572872 | tf_op jit(solution)/shard_map/ppermute | solution.py:91
  26.6 6.0 %collective-permute-start.10 = (bf16[128,512]{1,0:T(8,128)(2,1)S(1)}, bf16[128,512]{1,0:T(8,128)(2,1)S(1)}, u32[]{:S(2)}, u32[]{:S(2)}) collective-permute-start(bf16[128,512]{1,0:T(8,128)(2,1)S(1)} %slice.9), channel_id=1, source_target_pairs={{0,1},{2,0},{4,2},{6,4},{7,6},{5,7},{3,5},{1,3},{8,9},{10,8},{12,1... | collective-permute-start | bytes 393224 | tf_op jit(solution)/shard_map/ppermute | solution.py:45
  27.2 5.7 %collective-permute-start.9 = (bf16[128,512]{1,0:T(8,128)(2,1)S(1)}, bf16[128,512]{1,0:T(8,128)(2,1)S(1)}, u32[]{:S(2)}, u32[]{:S(2)}) collective-permute-start(bf16[128,512]{1,0:T(8,128)(2,1)S(1)} %slice.8), channel_id=1, source_target_pairs={{0,2},{2,4},{4,6},{6,7},{7,5},{5,3},{3,1},{1,0},{8,10},{10,12},{12... | collective-permute-start | bytes 393224 | tf_op jit(solution)/shard_map/ppermute | solution.py:45
  33.4 1.9 %collective-permute-start.11 = (bf16[128,384]{1,0:T(8,128)(2,1)S(1)}, bf16[128,384]{1,0:T(8,128)(2,1)S(1)}, u32[]{:S(2)}, u32[]{:S(2)}) collective-permute-start(bf16[128,384]{1,0:T(8,128)(2,1)S(1)} %get-tuple-element.38), channel_id=1, source_target_pairs={{0,8},{8,0},{16,24},{24,16},{1,9},{9,1},{17,25},{25,17},{2,10},{10... | collective-permute-start | bytes 294920 | tf_op jit(solution)/shard_map/ppermute | solution.py:349
  33.4 5.7 %collective-permute-start.12 = (bf16[128,384]{1,0:T(8,128)(2,1)S(1)}, bf16[128,384]{1,0:T(8,128)(2,1)S(1)}, u32[]{:S(2)}, u32[]{:S(2)}) collective-permute-start(bf16[128,384]{1,0:T(8,128)(2,1)S(1)} %get-tuple-element.39), channel_id=1, source_target_pairs={{0,16},{8,24},{16,0},{24,8},{1,17},{9,25},{17,1},{25,9},{2,18},{10... | collective-permute-start | bytes 294920 | tf_op jit(solution)/shard_map/ppermute | solution.py:349
  34.9 5.4 %collective-permute-start.13 = (bf16[128,384]{1,0:T(8,128)(2,1)S(1)}, bf16[128,384]{1,0:T(8,128)(2,1)S(1)}, u32[]{:S(2)}, u32[]{:S(2)}) collective-permute-start(bf16[128,384]{1,0:T(8,128)(2,1)S(1)} %get-tuple-element.40), channel_id=1, source_target_pairs={{0,24},{8,16},{16,8},{24,0},{1,25},{9,17},{17,9},{25,1},{2,26},{10... | collective-permute-start | bytes 294920 | tf_op jit(solution)/shard_map/ppermute | solution.py:349
  40.3 14.1 %collective-permute-start.21 = (bf16[512,512]{1,0:T(8,128)(2,1)S(1)}, bf16[512,512]{1,0:T(8,128)(2,1)S(1)}, u32[]{:S(2)}, u32[]{:S(2)}) collective-permute-start(bf16[512,512]{1,0:T(8,128)(2,1)S(1)} %get-tuple-element.44.refs_5_), channel_id=1, source_target_pairs={{0,16},{8,24},{16,0},{24,8},{1,17},{9,25},{17,1},{25,9},{2,18},{10... | collective-permute-start | bytes 1572872 | tf_op jit(solution)/shard_map/ppermute | solution.py:91
  41.9 5.8 %collective-permute-start.14 = (bf16[144,512]{1,0:T(8,128)(2,1)S(1)}, bf16[144,512]{1,0:T(8,128)(2,1)S(1)}, u32[]{:S(2)}, u32[]{:S(2)}) collective-permute-start(bf16[144,512]{1,0:T(8,128)(2,1)S(1)} %get-tuple-element.41.refs_0_.own), channel_id=1, source_target_pairs={{0,2},{2,4},{4,6},{6,7},{7,5},{5,3},{3,1},{1,0},{8,10},{10,12},{12... | collective-permute-start | bytes 442376 | tf_op jit(solution)/shard_map/ppermute | solution.py:53
  43.5 5.8 %collective-permute-start.17 = (bf16[144,512]{1,0:T(8,128)(2,1)S(1)}, bf16[144,512]{1,0:T(8,128)(2,1)S(1)}, u32[]{:S(2)}, u32[]{:S(2)}) collective-permute-start(bf16[144,512]{1,0:T(8,128)(2,1)S(1)} %get-tuple-element.41.refs_0_.own), channel_id=1, source_target_pairs={{0,1},{2,0},{4,2},{6,4},{7,6},{5,7},{3,5},{1,3},{8,9},{10,8},{12,1... | collective-permute-start | bytes 442376 | tf_op jit(solution)/shard_map/ppermute | solution.py:53
  47.7 5.1 %collective-permute-start.15 = (bf16[144,512]{1,0:T(8,128)(2,1)S(1)}, bf16[144,512]{1,0:T(8,128)(2,1)S(1)}, u32[]{:S(2)}, u32[]{:S(2)}) collective-permute-start(bf16[144,512]{1,0:T(8,128)(2,1)S(1)} %collective-permute-done.14.refs_1_), channel_id=1, source_target_pairs={{0,2},{2,4},{4,6},{6,7},{7,5},{5,3},{3,1},{1,0},{8,10},{10,12},{12... | collective-permute-start | bytes 442376 | tf_op jit(solution)/shard_map/ppermute | solution.py:53
  49.3 5.1 %collective-permute-start.18 = (bf16[144,512]{1,0:T(8,128)(2,1)S(1)}, bf16[144,512]{1,0:T(8,128)(2,1)S(1)}, u32[]{:S(2)}, u32[]{:S(2)}) collective-permute-start(bf16[144,512]{1,0:T(8,128)(2,1)S(1)} %collective-permute-done.17.refs_2_), channel_id=1, source_target_pairs={{0,1},{2,0},{4,2},{6,4},{7,6},{5,7},{3,5},{1,3},{8,9},{10,8},{12,1... | collective-permute-start | bytes 442376 | tf_op jit(solution)/shard_map/ppermute | solution.py:53
  49.7 6.7 %collective-permute-start.20 = (bf16[512,512]{1,0:T(8,128)(2,1)S(1)}, bf16[512,512]{1,0:T(8,128)(2,1)S(1)}, u32[]{:S(2)}, u32[]{:S(2)}) collective-permute-start(bf16[512,512]{1,0:T(8,128)(2,1)S(1)} %get-tuple-element.44.refs_5_), channel_id=1, source_target_pairs={{0,8},{8,0},{16,24},{24,16},{1,9},{9,1},{17,25},{25,17},{2,10},{10... | collective-permute-start | bytes 1572872 | tf_op jit(solution)/shard_map/ppermute | solution.py:91
  54.4 2.0 %collective-permute-start.22 = (bf16[512,512]{1,0:T(8,128)(2,1)S(1)}, bf16[512,512]{1,0:T(8,128)(2,1)S(1)}, u32[]{:S(2)}, u32[]{:S(2)}) collective-permute-start(bf16[512,512]{1,0:T(8,128)(2,1)S(1)} %collective-permute-done.21.refs_7_), channel_id=1, source_target_pairs={{0,8},{8,0},{16,24},{24,16},{1,9},{9,1},{17,25},{25,17},{2,10},{10... | collective-permute-start | bytes 1572872 | tf_op jit(solution)/shard_map/ppermute | solution.py:91
  54.4 6.3 %collective-permute-start.16 = (bf16[144,512]{1,0:T(8,128)(2,1)S(1)}, bf16[144,512]{1,0:T(8,128)(2,1)S(1)}, u32[]{:S(2)}, u32[]{:S(2)}) collective-permute-start(bf16[144,512]{1,0:T(8,128)(2,1)S(1)} %collective-permute-done.15.refs_3_), channel_id=1, source_target_pairs={{0,2},{2,4},{4,6},{6,7},{7,5},{5,3},{3,1},{1,0},{8,10},{10,12},{12... | collective-permute-start | bytes 442376 | tf_op jit(solution)/shard_map/ppermute | solution.py:53
  56.0 6.0 %collective-permute-start.19 = (bf16[144,512]{1,0:T(8,128)(2,1)S(1)}, bf16[144,512]{1,0:T(8,128)(2,1)S(1)}, u32[]{:S(2)}, u32[]{:S(2)}) collective-permute-start(bf16[144,512]{1,0:T(8,128)(2,1)S(1)} %collective-permute-done.18.refs_4_), channel_id=1, source_target_pairs={{0,1},{2,0},{4,2},{6,4},{7,6},{5,7},{3,5},{1,3},{8,9},{10,8},{12,1... | collective-permute-start | bytes 442376 | tf_op jit(solution)/shard_map/ppermute | solution.py:53
  62.0 5.2 %collective-permute-start.23 = (bf16[144,512]{1,0:T(8,128)(2,1)S(1)}, bf16[144,512]{1,0:T(8,128)(2,1)S(1)}, u32[]{:S(2)}, u32[]{:S(2)}) collective-permute-start(bf16[144,512]{1,0:T(8,128)(2,1)S(1)} %broadcast_select_fusion), channel_id=1, source_target_pairs={{0,2},{2,4},{4,6},{6,7},{7,5},{5,3},{3,1},{1,0},{8,9},{10,8},{12,1... | collective-permute-start | bytes 442376 | tf_op jit(solution)/shard_map/ppermute | solution.py:63
  (5 other events, 30.2 us)
